TPU v7x, 32 devices: a whole 2x2x4 slice. The times are simulated.
32 devices in a mesh: groups: 2 (over y), gx: 16 (over z, x, core).
Axes of the slice: x: 2, y: 2, z: 4, core: 2. Of those that a mesh axis runs over, the one named last changes fastest.
Arguments:
- temp0: float32 [32, 32, 1024], P(('groups', 'gx')), parts along dimension 0, may hold values from 0.3 to 1.6
- kappa: float32 [32, 32, 1024], P(('groups', 'gx')), parts along dimension 0, may hold values from 0.5 to 1.5
- act_step: int32 [32, 32, 1024], P(('groups', 'gx')), parts along dimension 0, may hold values from 0 to 4
- hface: float32 [32, 1024], P(('groups', 'gx')), parts along dimension 0, may hold values from 0.2 to 2
- codes: int32 [32, 1024], P(('groups', 'gx')), parts along dimension 0, may hold values from 0 to 2
- path: int32 [8, 32], P('groups'), parts along dimension 0, may hold values from 0 to 16383
- cotangent: float32 [32, 32, 1024], P(('groups', 'gx')), parts along dimension 0, may hold values from -6 to 6
Outputs:
- adjoint: float32 [32, 32, 1024], P(('groups', 'gx')), parts along dimension 0
- kappa_grad: float32 [32, 32, 1024], P(('groups', 'gx')), parts along dimension 0
- hface_grad: float32 [32, 1024], P(('groups', 'gx')), parts along dimension 0
There are 2 independent parts, one for each index of `groups`. A program takes and returns all parts, laid end to end along the dimension named above; each array names one. Nothing has to cross between parts.
All inputs are finite; a program needn't handle non-finite values.
Results may differ from a plain program's by a relative error of at most 0.0003.
Values sent between devices are 32-bit elements; how exact they have to be, the bound alone decides.
No kernel may reach another device: no remote copies, remote signals or barrier semaphores. Data moves between devices by JAX's collectives and lax.ppermute only.
A program may use at most 64 MiB of HBM per device.

v0:
```python
import jax
import jax.numpy as jnp
from jax import lax
from jax.sharding import PartitionSpec as P

LATENT = 1.5
MELT = 1.0
SPREAD = 0.15
DELTA = 0.05
EMISSION = 0.1
POWER = 8.0
AMBIENT = 0.2
SUBSTRATE = 0.5


def extended_2(cells, sides, width):
    for axis, dim in sides:
        count = lax.axis_size(axis)
        ends = count - 1
        head = lax.slice_in_dim(cells, 0, width, axis=dim)
        tail = lax.slice_in_dim(cells, cells.shape[dim] - width, cells.shape[dim], axis=dim)
        cells = jnp.concatenate(
            [
                lax.ppermute(tail, axis, [(i, (i + 1) % count) for i in range(ends)]),
                cells,
                lax.ppermute(head, axis, [((i + 1) % count, i) for i in range(ends)]),
            ],
            axis=dim,
        )
    return cells


def from_behind(value, axis, steps):
    count = lax.axis_size(axis)
    first, last = (max(0, -steps), min(count, count - steps))
    return lax.ppermute(value, axis, [(source, source + steps) for source in range(first, last)])


def conductivity(temp, kappa, active):
    return kappa * (1.0 + 0.5 * temp) * (0.1 + 0.9 * active)


def capacity(temp):
    return 1.0 + LATENT * jnp.exp(-jnp.square((temp - MELT) / SPREAD))


def harmonic(first, second):
    total = first + second
    return 2.0 * first * second / jnp.where(total > 0, total, 1.0)


def heating(spots, offset, planes, cols):
    xs = offset + lax.broadcasted_iota(jnp.int32, (1, planes, cols), 1)
    ys = lax.broadcasted_iota(jnp.int32, (1, planes, cols), 2)
    cells = xs * cols + ys
    hits = (spots[:, None, None] == cells).astype(jnp.float32)
    return POWER * jnp.sum(hits, axis=0)


def advance(temp_ext, keff_ext, hface, codes, heat):
    pads = ((0, 0), (1, 1), (1, 1))
    tpad = jnp.pad(temp_ext, pads)
    kpad = jnp.pad(keff_ext, pads)
    center = tpad[1:-1, 1:-1, 1:-1]
    kcen = kpad[1:-1, 1:-1, 1:-1]
    flux = jnp.zeros_like(center)
    slices = [
        (slice(2, None), slice(1, -1), slice(1, -1)),
        (slice(None, -2), slice(1, -1), slice(1, -1)),
        (slice(1, -1), slice(2, None), slice(1, -1)),
        (slice(1, -1), slice(None, -2), slice(1, -1)),
        (slice(1, -1), slice(1, -1), slice(2, None)),
        (slice(1, -1), slice(1, -1), slice(None, -2)),
    ]
    for place in slices:
        flux = flux + harmonic(kcen, kpad[place]) * (tpad[place] - center)
    top = center[:, 0, :]
    fourth = top * top * top * top
    loss = jnp.where(
        codes == 0,
        hface * (top - AMBIENT),
        jnp.where(codes == 1, EMISSION * hface * (fourth - AMBIENT**4), hface * (top - SUBSTRATE)),
    )
    surface = heat - loss
    depth = lax.broadcasted_iota(jnp.int32, (1, center.shape[1], 1), 1)
    flux = flux + jnp.where(depth == 0, surface[:, None, :], 0.0)
    return center + DELTA * flux / capacity(center)


def local_step(temp, kappa, active, lower, upper, hface, codes, heat):
    keff = conductivity(temp, kappa, active)
    temp_ext = jnp.concatenate([lower[0][None], temp, upper[0][None]], axis=0)
    keff_ext = jnp.concatenate([lower[1][None], keff, upper[1][None]], axis=0)
    return advance(temp_ext, keff_ext, hface, codes, heat)


def edges(temp, kappa, active):
    keff = conductivity(temp, kappa, active)
    return (jnp.stack([temp[0], keff[0]]), jnp.stack([temp[-1], keff[-1]]))


def rim_pair(temp, kappa, active):
    keff = conductivity(temp, kappa, active)
    extended = extended_2(jnp.stack([temp, keff]), (("gx", 1),), 1)
    return (extended[:, 0], extended[:, -1])


def body(temp0, kappa, act_step, hface, codes, path, cotangent):
    planes = temp0.shape[0]
    cols = temp0.shape[2]
    offset = lax.axis_index("gx") * planes
    steps_count = path.shape[0]
    temps = [temp0]
    stored = []
    temp = temp0
    for step in range(steps_count):
        active = (act_step <= step).astype(jnp.float32)
        lower, upper = rim_pair(temp, kappa, active)
        stored.append((lower, upper))
        heat = heating(path[step], offset, planes, cols)
        temp = local_step(temp, kappa, active, lower, upper, hface, codes, heat)
        temps.append(temp)
    adjoint = cotangent
    kappa_grad = jnp.zeros_like(kappa)
    hface_grad = jnp.zeros_like(hface)
    for step in reversed(range(steps_count)):
        temp = temps[step]
        active = (act_step <= step).astype(jnp.float32)
        heat = heating(path[step], offset, planes, cols)
        lower, upper = rim_pair(temp, kappa, active)

        def stepper(temp_in, kappa_in, hface_in, lower_in, upper_in):
            return local_step(temp_in, kappa_in, active, lower_in, upper_in, hface_in, codes, heat)

        result, pull = jax.vjp(stepper, temp, kappa, hface, lower, upper)
        dtemp, dkappa, dhface, dlower, dupper = pull(adjoint)
        from_above = from_behind(dlower, "gx", -1)
        from_below = from_behind(dupper, "gx", 1)

        def rimmer(temp_in, kappa_in):
            return edges(temp_in, kappa_in, active)

        rim_out, pull_edge = jax.vjp(rimmer, temp, kappa)
        etemp, ekappa = pull_edge((from_below, from_above))
        adjoint = dtemp + etemp
        kappa_grad = kappa_grad + dkappa + ekappa
        hface_grad = hface_grad + dhface
    return (adjoint, kappa_grad, hface_grad)


def solution(mesh):
    placed = (
        P(("groups", "gx"), None, None),
        P(("groups", "gx"), None, None),
        P(("groups", "gx"), None, None),
        P(("groups", "gx"), None),
        P(("groups", "gx"), None),
        P("groups", None),
        P(("groups", "gx"), None, None),
    )
    return jax.shard_map(
        body,
        mesh=mesh,
        in_specs=placed,
        out_specs=(
            P(("groups", "gx"), None, None),
            P(("groups", "gx"), None, None),
            P(("groups", "gx"), None),
        ),
        check_vma=False,
    )
```

profile of v0, /device:TPU:3, one launch (start us, length us, event | category | flops | bytes accessed | tf_op | source)
XLA Modules:
  0.0 103.0 jit_solution(11073138425141099464)
XLA Ops:
  0.6 1.1 %fusion.23 = (f32[1,32,1024]{2,1,0:T(8,128)S(1)}, pred[1,32,1024]{2,1,0:T(8,128)(4,1)S(1)}) fusion(f32[1,32,1024]{2,1,0:T(8,128)} %param.8, f32[1,32,1024]{2,1,0:T(8,128)} %param.7, s32[1,32,1024]{2,1,0:T(8,128)} %param.9), kind=kLoop, calls=%fused_computation.273 | loop fusion | flops 229376 | bytes 557056 | tf_op jit(solution)/shard_map/mul | solution.py:40
  1.8 2.6 %collective-permute-start.1 = (f32[2,1,32,1024]{3,2,1,0:T(8,128)S(1)}, f32[2,1,32,1024]{3,2,1,0:T(8,128)S(1)}, u32[]{:S(2)}, u32[]{:S(2)}) collective-permute-start(f32[2,1,32,1024]{3,2,1,0:T(8,128)S(1)} %pad_maximum_fusion), channel_id=1, source_target_pairs={{1,0},{2,1},{3,2},{4,3},{5,4},{6,5},{7,6},{8,7},{9,8},{10,9},{11,1... | collective-permute-start | bytes 786440 | tf_op jit(solution)/shard_map/ppermute | solution.py:26
  4.4 3.9 %collective-permute-start = (f32[2,1,32,1024]{3,2,1,0:T(8,128)S(1)}, f32[2,1,32,1024]{3,2,1,0:T(8,128)S(1)}, u32[]{:S(2)}, u32[]{:S(2)}) collective-permute-start(f32[2,1,32,1024]{3,2,1,0:T(8,128)S(1)} %pad_maximum_fusion), channel_id=1, source_target_pairs={{0,1},{1,2},{2,3},{3,4},{4,5},{5,6},{6,7},{7,8},{8,9},{9,10},{10,1... | collective-permute-start | bytes 786440 | tf_op jit(solution)/shard_map/ppermute | solution.py:24
  10.5 1.1 %collective-permute-done = f32[2,1,32,1024]{3,2,1,0:T(8,128)S(1)} collective-permute-done((f32[2,1,32,1024]{3,2,1,0:T(8,128)S(1)}, f32[2,1,32,1024]{3,2,1,0:T(8,128)S(1)}, u32[]{:S(2)}, u32[]{:S(2)}) %collective-permute-start) | collective-permute-done | bytes 262176 | tf_op jit(solution)/shard_map/ppermute | solution.py:24
  13.1 4.2 %collective-permute-start.3 = (f32[2,1,32,1024]{3,2,1,0:T(8,128)S(1)}, f32[2,1,32,1024]{3,2,1,0:T(8,128)S(1)}, u32[]{:S(2)}, u32[]{:S(2)}) collective-permute-start(f32[2,1,32,1024]{3,2,1,0:T(8,128)S(1)} %pad_maximum_fusion.1), channel_id=1, source_target_pairs={{1,0},{2,1},{3,2},{4,3},{5,4},{6,5},{7,6},{8,7},{9,8},{10,9},{11,1... | collective-permute-start | bytes 786440 | tf_op jit(solution)/shard_map/ppermute | solution.py:26
  17.3 3.0 %collective-permute-start.2 = (f32[2,1,32,1024]{3,2,1,0:T(8,128)S(1)}, f32[2,1,32,1024]{3,2,1,0:T(8,128)S(1)}, u32[]{:S(2)}, u32[]{:S(2)}) collective-permute-start(f32[2,1,32,1024]{3,2,1,0:T(8,128)S(1)} %pad_maximum_fusion.1), channel_id=1, source_target_pairs={{0,1},{1,2},{2,3},{3,4},{4,5},{5,6},{6,7},{7,8},{8,9},{9,10},{10,1... | collective-permute-start | bytes 786440 | tf_op jit(solution)/shard_map/ppermute | solution.py:24
  20.3 2.2 %collective-permute-done.3 = f32[2,1,32,1024]{3,2,1,0:T(8,128)S(1)} collective-permute-done((f32[2,1,32,1024]{3,2,1,0:T(8,128)S(1)}, f32[2,1,32,1024]{3,2,1,0:T(8,128)S(1)}, u32[]{:S(2)}, u32[]{:S(2)}) %collective-permute-start.3) | collective-permute-done | bytes 262176 | tf_op jit(solution)/shard_map/ppermute | solution.py:26
  22.5 1.1 %collective-permute-done.2 = f32[2,1,32,1024]{3,2,1,0:T(8,128)S(1)} collective-permute-done((f32[2,1,32,1024]{3,2,1,0:T(8,128)S(1)}, f32[2,1,32,1024]{3,2,1,0:T(8,128)S(1)}, u32[]{:S(2)}, u32[]{:S(2)}) %collective-permute-start.2) | collective-permute-done | bytes 262176 | tf_op jit(solution)/shard_map/ppermute | solution.py:24
  24.6 4.2 %collective-permute-start.5 = (f32[2,1,32,1024]{3,2,1,0:T(8,128)S(1)}, f32[2,1,32,1024]{3,2,1,0:T(8,128)S(1)}, u32[]{:S(2)}, u32[]{:S(2)}) collective-permute-start(f32[2,1,32,1024]{3,2,1,0:T(8,128)S(1)} %pad_maximum_fusion.2), channel_id=1, source_target_pairs={{1,0},{2,1},{3,2},{4,3},{5,4},{6,5},{7,6},{8,7},{9,8},{10,9},{11,1... | collective-permute-start | bytes 786440 | tf_op jit(solution)/shard_map/ppermute | solution.py:26
  28.8 3.1 %collective-permute-start.4 = (f32[2,1,32,1024]{3,2,1,0:T(8,128)S(1)}, f32[2,1,32,1024]{3,2,1,0:T(8,128)S(1)}, u32[]{:S(2)}, u32[]{:S(2)}) collective-permute-start(f32[2,1,32,1024]{3,2,1,0:T(8,128)S(1)} %pad_maximum_fusion.2), channel_id=1, source_target_pairs={{0,1},{1,2},{2,3},{3,4},{4,5},{5,6},{6,7},{7,8},{8,9},{9,10},{10,1... | collective-permute-start | bytes 786440 | tf_op jit(solution)/shard_map/ppermute | solution.py:24
  31.9 2.2 %collective-permute-done.5 = f32[2,1,32,1024]{3,2,1,0:T(8,128)S(1)} collective-permute-done((f32[2,1,32,1024]{3,2,1,0:T(8,128)S(1)}, f32[2,1,32,1024]{3,2,1,0:T(8,128)S(1)}, u32[]{:S(2)}, u32[]{:S(2)}) %collective-permute-start.5) | collective-permute-done | bytes 262176 | tf_op jit(solution)/shard_map/ppermute | solution.py:26
  34.1 1.1 %collective-permute-done.4 = f32[2,1,32,1024]{3,2,1,0:T(8,128)S(1)} collective-permute-done((f32[2,1,32,1024]{3,2,1,0:T(8,128)S(1)}, f32[2,1,32,1024]{3,2,1,0:T(8,128)S(1)}, u32[]{:S(2)}, u32[]{:S(2)}) %collective-permute-start.4) | collective-permute-done | bytes 262176 | tf_op jit(solution)/shard_map/ppermute | solution.py:24
  36.2 4.2 %collective-permute-start.7 = (f32[2,1,32,1024]{3,2,1,0:T(8,128)S(1)}, f32[2,1,32,1024]{3,2,1,0:T(8,128)S(1)}, u32[]{:S(2)}, u32[]{:S(2)}) collective-permute-start(f32[2,1,32,1024]{3,2,1,0:T(8,128)S(1)} %pad_maximum_fusion.3), channel_id=1, source_target_pairs={{1,0},{2,1},{3,2},{4,3},{5,4},{6,5},{7,6},{8,7},{9,8},{10,9},{11,1... | collective-permute-start | bytes 786440 | tf_op jit(solution)/shard_map/ppermute | solution.py:26
  40.4 3.1 %collective-permute-start.6 = (f32[2,1,32,1024]{3,2,1,0:T(8,128)S(1)}, f32[2,1,32,1024]{3,2,1,0:T(8,128)S(1)}, u32[]{:S(2)}, u32[]{:S(2)}) collective-permute-start(f32[2,1,32,1024]{3,2,1,0:T(8,128)S(1)} %pad_maximum_fusion.3), channel_id=1, source_target_pairs={{0,1},{1,2},{2,3},{3,4},{4,5},{5,6},{6,7},{7,8},{8,9},{9,10},{10,1... | collective-permute-start | bytes 786440 | tf_op jit(solution)/shard_map/ppermute | solution.py:24
  43.5 2.2 %collective-permute-done.7 = f32[2,1,32,1024]{3,2,1,0:T(8,128)S(1)} collective-permute-done((f32[2,1,32,1024]{3,2,1,0:T(8,128)S(1)}, f32[2,1,32,1024]{3,2,1,0:T(8,128)S(1)}, u32[]{:S(2)}, u32[]{:S(2)}) %collective-permute-start.7) | collective-permute-done | bytes 262176 | tf_op jit(solution)/shard_map/ppermute | solution.py:26
  45.8 1.1 %collective-permute-done.6 = f32[2,1,32,1024]{3,2,1,0:T(8,128)S(1)} collective-permute-done((f32[2,1,32,1024]{3,2,1,0:T(8,128)S(1)}, f32[2,1,32,1024]{3,2,1,0:T(8,128)S(1)}, u32[]{:S(2)}, u32[]{:S(2)}) %collective-permute-start.6) | collective-permute-done | bytes 262176 | tf_op jit(solution)/shard_map/ppermute | solution.py:24
  49.6 5.3 %collective-permute-start.9 = (f32[2,32,1024]{2,1,0:T(8,128)S(1)}, f32[2,32,1024]{2,1,0:T(8,128)S(1)}, u32[]{:S(2)}, u32[]{:S(2)}) collective-permute-start(f32[2,32,1024]{2,1,0:T(8,128)S(1)} %pad_add_fusion.6), channel_id=1, source_target_pairs={{0,1},{1,2},{2,3},{3,4},{4,5},{5,6},{6,7},{7,8},{8,9},{9,10},{10,1... | collective-permute-start | bytes 786440 | tf_op jit(solution)/shard_map/ppermute | solution.py:36
  55.0 1.9 %collective-permute-start.8 = (f32[2,32,1024]{2,1,0:T(8,128)S(1)}, f32[2,32,1024]{2,1,0:T(8,128)S(1)}, u32[]{:S(2)}, u32[]{:S(2)}) collective-permute-start(f32[2,32,1024]{2,1,0:T(8,128)S(1)} %pad_add_fusion.7), channel_id=1, source_target_pairs={{1,0},{2,1},{3,2},{4,3},{5,4},{6,5},{7,6},{8,7},{9,8},{10,9},{11,1... | collective-permute-start | bytes 786440 | tf_op jit(solution)/shard_map/ppermute | solution.py:36
  56.9 1.3 %collective-permute-done.9 = f32[2,32,1024]{2,1,0:T(8,128)S(1)} collective-permute-done((f32[2,32,1024]{2,1,0:T(8,128)S(1)}, f32[2,32,1024]{2,1,0:T(8,128)S(1)}, u32[]{:S(2)}, u32[]{:S(2)}) %collective-permute-start.9) | collective-permute-done | bytes 262176 | tf_op jit(solution)/shard_map/ppermute | solution.py:36
  58.3 5.3 %collective-permute-done.8 = f32[2,32,1024]{2,1,0:T(8,128)S(1)} collective-permute-done((f32[2,32,1024]{2,1,0:T(8,128)S(1)}, f32[2,32,1024]{2,1,0:T(8,128)S(1)}, u32[]{:S(2)}, u32[]{:S(2)}) %collective-permute-start.8) | collective-permute-done | bytes 262176 | tf_op jit(solution)/shard_map/ppermute | solution.py:36
  65.4 1.9 %collective-permute-start.11 = (f32[2,32,1024]{2,1,0:T(8,128)S(1)}, f32[2,32,1024]{2,1,0:T(8,128)S(1)}, u32[]{:S(2)}, u32[]{:S(2)}) collective-permute-start(f32[2,32,1024]{2,1,0:T(8,128)S(1)} %pad_add_fusion.4), channel_id=1, source_target_pairs={{0,1},{1,2},{2,3},{3,4},{4,5},{5,6},{6,7},{7,8},{8,9},{9,10},{10,1... | collective-permute-start | bytes 786440 | tf_op jit(solution)/shard_map/ppermute | solution.py:36
  67.3 2.4 %collective-permute-start.10 = (f32[2,32,1024]{2,1,0:T(8,128)S(1)}, f32[2,32,1024]{2,1,0:T(8,128)S(1)}, u32[]{:S(2)}, u32[]{:S(2)}) collective-permute-start(f32[2,32,1024]{2,1,0:T(8,128)S(1)} %pad_add_fusion.5), channel_id=1, source_target_pairs={{1,0},{2,1},{3,2},{4,3},{5,4},{6,5},{7,6},{8,7},{9,8},{10,9},{11,1... | collective-permute-start | bytes 786440 | tf_op jit(solution)/shard_map/ppermute | solution.py:36
  69.8 0.9 collective-permute-done.11
  70.6 5.3 %collective-permute-done.10 = f32[2,32,1024]{2,1,0:T(8,128)S(1)} collective-permute-done((f32[2,32,1024]{2,1,0:T(8,128)S(1)}, f32[2,32,1024]{2,1,0:T(8,128)S(1)}, u32[]{:S(2)}, u32[]{:S(2)}) %collective-permute-start.10) | collective-permute-done | bytes 262176 | tf_op jit(solution)/shard_map/ppermute | solution.py:36
  77.7 1.9 %collective-permute-start.13 = (f32[2,32,1024]{2,1,0:T(8,128)S(1)}, f32[2,32,1024]{2,1,0:T(8,128)S(1)}, u32[]{:S(2)}, u32[]{:S(2)}) collective-permute-start(f32[2,32,1024]{2,1,0:T(8,128)S(1)} %pad_add_fusion.2), channel_id=1, source_target_pairs={{0,1},{1,2},{2,3},{3,4},{4,5},{5,6},{6,7},{7,8},{8,9},{9,10},{10,1... | collective-permute-start | bytes 786440 | tf_op jit(solution)/shard_map/ppermute | solution.py:36
  79.7 2.6 %collective-permute-start.12 = (f32[2,32,1024]{2,1,0:T(8,128)S(1)}, f32[2,32,1024]{2,1,0:T(8,128)S(1)}, u32[]{:S(2)}, u32[]{:S(2)}) collective-permute-start(f32[2,32,1024]{2,1,0:T(8,128)S(1)} %pad_add_fusion.3), channel_id=1, source_target_pairs={{1,0},{2,1},{3,2},{4,3},{5,4},{6,5},{7,6},{8,7},{9,8},{10,9},{11,1... | collective-permute-start | bytes 786440 | tf_op jit(solution)/shard_map/ppermute | solution.py:36
  82.9 5.3 %collective-permute-done.12 = f32[2,32,1024]{2,1,0:T(8,128)S(1)} collective-permute-done((f32[2,32,1024]{2,1,0:T(8,128)S(1)}, f32[2,32,1024]{2,1,0:T(8,128)S(1)}, u32[]{:S(2)}, u32[]{:S(2)}) %collective-permute-start.12) | collective-permute-done | bytes 262176 | tf_op jit(solution)/shard_map/ppermute | solution.py:36
  90.7 1.9 %collective-permute-start.15 = (f32[2,32,1024]{2,1,0:T(8,128)S(1)}, f32[2,32,1024]{2,1,0:T(8,128)S(1)}, u32[]{:S(2)}, u32[]{:S(2)}) collective-permute-start(f32[2,32,1024]{2,1,0:T(8,128)S(1)} %pad_add_fusion), channel_id=1, source_target_pairs={{0,1},{1,2},{2,3},{3,4},{4,5},{5,6},{6,7},{7,8},{8,9},{9,10},{10,1... | collective-permute-start | bytes 786440 | tf_op jit(solution)/shard_map/ppermute | solution.py:36
  92.6 2.4 %collective-permute-start.14 = (f32[2,32,1024]{2,1,0:T(8,128)S(1)}, f32[2,32,1024]{2,1,0:T(8,128)S(1)}, u32[]{:S(2)}, u32[]{:S(2)}) collective-permute-start(f32[2,32,1024]{2,1,0:T(8,128)S(1)} %pad_add_fusion.1), channel_id=1, source_target_pairs={{1,0},{2,1},{3,2},{4,3},{5,4},{6,5},{7,6},{8,7},{9,8},{10,9},{11,1... | collective-permute-start | bytes 786440 | tf_op jit(solution)/shard_map/ppermute | solution.py:36
  95.1 0.9 collective-permute-done.15
  95.9 5.3 %collective-permute-done.14 = f32[2,32,1024]{2,1,0:T(8,128)S(1)} collective-permute-done((f32[2,32,1024]{2,1,0:T(8,128)S(1)}, f32[2,32,1024]{2,1,0:T(8,128)S(1)}, u32[]{:S(2)}, u32[]{:S(2)}) %collective-permute-start.14) | collective-permute-done | bytes 262176 | tf_op jit(solution)/shard_map/ppermute | solution.py:36
  101.2 1.0 fusion.19
  (90 shorter events, 15.9 us)
Async XLA Ops:
  0.6 1.1 %copy-start = (f32[1,32,1024]{2,1,0:T(8,128)S(1)}, f32[1,32,1024]{2,1,0:T(8,128)}, u32[]{:S(2)}) copy-start(f32[1,32,1024]{2,1,0:T(8,128)} %param.7) | copy-start | bytes 393220
  1.8 8.7 %collective-permute-start.1 = (f32[2,1,32,1024]{3,2,1,0:T(8,128)S(1)}, f32[2,1,32,1024]{3,2,1,0:T(8,128)S(1)}, u32[]{:S(2)}, u32[]{:S(2)}) collective-permute-start(f32[2,1,32,1024]{3,2,1,0:T(8,128)S(1)} %pad_maximum_fusion), channel_id=1, source_target_pairs={{1,0},{2,1},{3,2},{4,3},{5,4},{6,5},{7,6},{8,7},{9,8},{10,9},{11,1... | collective-permute-start | bytes 786440 | tf_op jit(solution)/shard_map/ppermute | solution.py:26
  4.4 7.2 %collective-permute-start = (f32[2,1,32,1024]{3,2,1,0:T(8,128)S(1)}, f32[2,1,32,1024]{3,2,1,0:T(8,128)S(1)}, u32[]{:S(2)}, u32[]{:S(2)}) collective-permute-start(f32[2,1,32,1024]{3,2,1,0:T(8,128)S(1)} %pad_maximum_fusion), channel_id=1, source_target_pairs={{0,1},{1,2},{2,3},{3,4},{4,5},{5,6},{6,7},{7,8},{8,9},{9,10},{10,1... | collective-permute-start | bytes 786440 | tf_op jit(solution)/shard_map/ppermute | solution.py:24
  8.3 0.7 copy-start.6
  9.1 0.7 copy-start.4
  9.1 0.7 copy-start.5
  11.6 0.9 copy-start.1
  11.6 1.0 copy-start.2
  13.1 9.4 %collective-permute-start.3 = (f32[2,1,32,1024]{3,2,1,0:T(8,128)S(1)}, f32[2,1,32,1024]{3,2,1,0:T(8,128)S(1)}, u32[]{:S(2)}, u32[]{:S(2)}) collective-permute-start(f32[2,1,32,1024]{3,2,1,0:T(8,128)S(1)} %pad_maximum_fusion.1), channel_id=1, source_target_pairs={{1,0},{2,1},{3,2},{4,3},{5,4},{6,5},{7,6},{8,7},{9,8},{10,9},{11,1... | collective-permute-start | bytes 786440 | tf_op jit(solution)/shard_map/ppermute | solution.py:26
  17.3 6.3 %collective-permute-start.2 = (f32[2,1,32,1024]{3,2,1,0:T(8,128)S(1)}, f32[2,1,32,1024]{3,2,1,0:T(8,128)S(1)}, u32[]{:S(2)}, u32[]{:S(2)}) collective-permute-start(f32[2,1,32,1024]{3,2,1,0:T(8,128)S(1)} %pad_maximum_fusion.1), channel_id=1, source_target_pairs={{0,1},{1,2},{2,3},{3,4},{4,5},{5,6},{6,7},{7,8},{8,9},{9,10},{10,1... | collective-permute-start | bytes 786440 | tf_op jit(solution)/shard_map/ppermute | solution.py:24
  24.6 9.5 %collective-permute-start.5 = (f32[2,1,32,1024]{3,2,1,0:T(8,128)S(1)}, f32[2,1,32,1024]{3,2,1,0:T(8,128)S(1)}, u32[]{:S(2)}, u32[]{:S(2)}) collective-permute-start(f32[2,1,32,1024]{3,2,1,0:T(8,128)S(1)} %pad_maximum_fusion.2), channel_id=1, source_target_pairs={{1,0},{2,1},{3,2},{4,3},{5,4},{6,5},{7,6},{8,7},{9,8},{10,9},{11,1... | collective-permute-start | bytes 786440 | tf_op jit(solution)/shard_map/ppermute | solution.py:26
  28.8 6.4 %collective-permute-start.4 = (f32[2,1,32,1024]{3,2,1,0:T(8,128)S(1)}, f32[2,1,32,1024]{3,2,1,0:T(8,128)S(1)}, u32[]{:S(2)}, u32[]{:S(2)}) collective-permute-start(f32[2,1,32,1024]{3,2,1,0:T(8,128)S(1)} %pad_maximum_fusion.2), channel_id=1, source_target_pairs={{0,1},{1,2},{2,3},{3,4},{4,5},{5,6},{6,7},{7,8},{8,9},{9,10},{10,1... | collective-permute-start | bytes 786440 | tf_op jit(solution)/shard_map/ppermute | solution.py:24
  36.2 9.5 %collective-permute-start.7 = (f32[2,1,32,1024]{3,2,1,0:T(8,128)S(1)}, f32[2,1,32,1024]{3,2,1,0:T(8,128)S(1)}, u32[]{:S(2)}, u32[]{:S(2)}) collective-permute-start(f32[2,1,32,1024]{3,2,1,0:T(8,128)S(1)} %pad_maximum_fusion.3), channel_id=1, source_target_pairs={{1,0},{2,1},{3,2},{4,3},{5,4},{6,5},{7,6},{8,7},{9,8},{10,9},{11,1... | collective-permute-start | bytes 786440 | tf_op jit(solution)/shard_map/ppermute | solution.py:26
  40.4 6.4 %collective-permute-start.6 = (f32[2,1,32,1024]{3,2,1,0:T(8,128)S(1)}, f32[2,1,32,1024]{3,2,1,0:T(8,128)S(1)}, u32[]{:S(2)}, u32[]{:S(2)}) collective-permute-start(f32[2,1,32,1024]{3,2,1,0:T(8,128)S(1)} %pad_maximum_fusion.3), channel_id=1, source_target_pairs={{0,1},{1,2},{2,3},{3,4},{4,5},{5,6},{6,7},{7,8},{8,9},{9,10},{10,1... | collective-permute-start | bytes 786440 | tf_op jit(solution)/shard_map/ppermute | solution.py:24
  47.1 0.9 copy-start.3
  49.6 8.7 %collective-permute-start.9 = (f32[2,32,1024]{2,1,0:T(8,128)S(1)}, f32[2,32,1024]{2,1,0:T(8,128)S(1)}, u32[]{:S(2)}, u32[]{:S(2)}) collective-permute-start(f32[2,32,1024]{2,1,0:T(8,128)S(1)} %pad_add_fusion.6), channel_id=1, source_target_pairs={{0,1},{1,2},{2,3},{3,4},{4,5},{5,6},{6,7},{7,8},{8,9},{9,10},{10,1... | collective-permute-start | bytes 786440 | tf_op jit(solution)/shard_map/ppermute | solution.py:36
  55.0 8.6 %collective-permute-start.8 = (f32[2,32,1024]{2,1,0:T(8,128)S(1)}, f32[2,32,1024]{2,1,0:T(8,128)S(1)}, u32[]{:S(2)}, u32[]{:S(2)}) collective-permute-start(f32[2,32,1024]{2,1,0:T(8,128)S(1)} %pad_add_fusion.7), channel_id=1, source_target_pairs={{1,0},{2,1},{3,2},{4,3},{5,4},{6,5},{7,6},{8,7},{9,8},{10,9},{11,1... | collective-permute-start | bytes 786440 | tf_op jit(solution)/shard_map/ppermute | solution.py:36
  65.4 5.2 %collective-permute-start.11 = (f32[2,32,1024]{2,1,0:T(8,128)S(1)}, f32[2,32,1024]{2,1,0:T(8,128)S(1)}, u32[]{:S(2)}, u32[]{:S(2)}) collective-permute-start(f32[2,32,1024]{2,1,0:T(8,128)S(1)} %pad_add_fusion.4), channel_id=1, source_target_pairs={{0,1},{1,2},{2,3},{3,4},{4,5},{5,6},{6,7},{7,8},{8,9},{9,10},{10,1... | collective-permute-start | bytes 786440 | tf_op jit(solution)/shard_map/ppermute | solution.py:36
  67.3 8.6 %collective-permute-start.10 = (f32[2,32,1024]{2,1,0:T(8,128)S(1)}, f32[2,32,1024]{2,1,0:T(8,128)S(1)}, u32[]{:S(2)}, u32[]{:S(2)}) collective-permute-start(f32[2,32,1024]{2,1,0:T(8,128)S(1)} %pad_add_fusion.5), channel_id=1, source_target_pairs={{1,0},{2,1},{3,2},{4,3},{5,4},{6,5},{7,6},{8,7},{9,8},{10,9},{11,1... | collective-permute-start | bytes 786440 | tf_op jit(solution)/shard_map/ppermute | solution.py:36
  77.7 5.2 %collective-permute-start.13 = (f32[2,32,1024]{2,1,0:T(8,128)S(1)}, f32[2,32,1024]{2,1,0:T(8,128)S(1)}, u32[]{:S(2)}, u32[]{:S(2)}) collective-permute-start(f32[2,32,1024]{2,1,0:T(8,128)S(1)} %pad_add_fusion.2), channel_id=1, source_target_pairs={{0,1},{1,2},{2,3},{3,4},{4,5},{5,6},{6,7},{7,8},{8,9},{9,10},{10,1... | collective-permute-start | bytes 786440 | tf_op jit(solution)/shard_map/ppermute | solution.py:36
  79.7 8.6 %collective-permute-start.12 = (f32[2,32,1024]{2,1,0:T(8,128)S(1)}, f32[2,32,1024]{2,1,0:T(8,128)S(1)}, u32[]{:S(2)}, u32[]{:S(2)}) collective-permute-start(f32[2,32,1024]{2,1,0:T(8,128)S(1)} %pad_add_fusion.3), channel_id=1, source_target_pairs={{1,0},{2,1},{3,2},{4,3},{5,4},{6,5},{7,6},{8,7},{9,8},{10,9},{11,1... | collective-permute-start | bytes 786440 | tf_op jit(solution)/shard_map/ppermute | solution.py:36
  90.7 5.2 %collective-permute-start.15 = (f32[2,32,1024]{2,1,0:T(8,128)S(1)}, f32[2,32,1024]{2,1,0:T(8,128)S(1)}, u32[]{:S(2)}, u32[]{:S(2)}) collective-permute-start(f32[2,32,1024]{2,1,0:T(8,128)S(1)} %pad_add_fusion), channel_id=1, source_target_pairs={{0,1},{1,2},{2,3},{3,4},{4,5},{5,6},{6,7},{7,8},{8,9},{9,10},{10,1... | collective-permute-start | bytes 786440 | tf_op jit(solution)/shard_map/ppermute | solution.py:36
  92.6 8.6 %collective-permute-start.14 = (f32[2,32,1024]{2,1,0:T(8,128)S(1)}, f32[2,32,1024]{2,1,0:T(8,128)S(1)}, u32[]{:S(2)}, u32[]{:S(2)}) collective-permute-start(f32[2,32,1024]{2,1,0:T(8,128)S(1)} %pad_add_fusion.1), channel_id=1, source_target_pairs={{1,0},{2,1},{3,2},{4,3},{5,4},{6,5},{7,6},{8,7},{9,8},{10,9},{11,1... | collective-permute-start | bytes 786440 | tf_op jit(solution)/shard_map/ppermute | solution.py:36
where the time goes:
time: 104 us; the launch traced here: 103 us
  starting transfers between devices  48.6 us (47%)
  waiting for transfers between devices  36.6 us (35%)
  other arithmetic  13.9 us (13%)
  local copies, waits for them, and re-layouts  2.78 us (3%)
  between operations  1.16 us (1%)
    ppermute x8, waiting for transfers between devices, from_behind(): lax.ppermute(value, axis, [(source, source + steps) for source in range(f...  25 us
    ppermute x8, starting transfers between devices, from_behind(): lax.ppermute(value, axis, [(source, source + steps) for source in range(f...  20.4 us
    ppermute x4, starting transfers between devices, extended_2(): lax.ppermute(head, axis, [((i + 1) % count, i) for i in range(ends)])  15.1 us
    ppermute x4, starting transfers between devices, extended_2(): lax.ppermute(tail, axis, [(i, (i + 1) % count) for i in range(ends)])  13.1 us
    ppermute x4, waiting for transfers between devices, extended_2(): lax.ppermute(head, axis, [((i + 1) % count, i) for i in range(ends)])  7.17 us
    ppermute x4, waiting for transfers between devices, extended_2(): lax.ppermute(tail, axis, [(i, (i + 1) % count) for i in range(ends)])  4.39 us
    add_any x9, other arithmetic, harmonic(): total = first + second  3.89 us
    unnamed x14, local copies, waits for them, and re-layouts  2.64 us
  transfers between devices with their start and end apart: 16, of which 16 were waited for; matrix products, arithmetic and copies ran while one was open for 0% of the time, Pallas kernels for 0%

commit v1 on v0

v1 whole, which is shorter than its diff:
```python
import math

import jax
import jax.numpy as jnp
from jax import lax
from jax.experimental import pallas as pl
from jax.experimental.pallas import tpu as pltpu
from jax.sharding import PartitionSpec as P

LATENT = 1.5
MELT = 1.0
SPREAD = 0.15
DELTA = 0.05
EMISSION = 0.1
POWER = 8.0
AMBIENT = 0.2
SUBSTRATE = 0.5

LANES = 128
HALF = 64
LEFT = 96
IN_ROWS = 88
OUT_ROWS = 40


def lane_iota(rows):
    return lax.broadcasted_iota(jnp.int32, (rows, LANES), 1)


def pack_kernel(parts, width, temp, kappa, act, hface, codes, cot, out):
    tiles = temp.shape[-1] // LANES

    def window(ref, start, rows):
        tile, off = divmod(start, LANES)

        def part(t):
            t = min(max(t, 0), tiles - 1)
            value = ref[0, :, t * LANES : (t + 1) * LANES] if len(ref.shape) == 3 else ref[:, t * LANES : (t + 1) * LANES]
            value = value.astype(jnp.float32)
            return value if off == 0 else pltpu.roll(value, LANES - off, axis=1)

        lane = lane_iota(rows)
        result = part(tile)
        if off > LANES - HALF - 7:
            result = jnp.where((lane >= LANES - off) & (lane < LEFT), part(tile + 1), result)
        if off < 7:
            result = jnp.where((lane >= LEFT) & (lane < LANES - off), part(tile - 1), result)
        return result

    rows = temp.shape[1]
    half = rows // 2
    lane = lane_iota(rows)
    for d in range(parts):
        start = d * width
        t = window(temp, start, rows)
        k = window(kappa, start, rows)
        a = window(act, start, rows)
        c = window(cot, start, rows)
        extra = jnp.where(
            lane >= 89,
            pltpu.roll(a, 96, axis=1),
            jnp.where(lane >= 75, pltpu.roll(c, 11, axis=1), pltpu.roll(c, 75, axis=1)),
        )
        out[d, 0:rows] = jnp.where((lane >= 71) & (lane < 121), extra, t)
        out[d, rows : 2 * rows] = jnp.where((lane >= 75) & (lane < 121), pltpu.roll(a, 50, axis=1), k)
        out[d, 2 * rows : 2 * rows + half] = jnp.where(
            lane[:half] < HALF, c[:half], pltpu.roll(c[half:], HALF, axis=1)
        )
        h = window(hface, start, 1)
        s = window(codes, start, 1)
        row = lax.broadcasted_iota(jnp.int32, (8, LANES), 0)
        out[d, 2 * rows + half : 2 * rows + half + 8] = jnp.where(row == 0, h, s)


def reciprocal(value):
    return 1.0 / value


def shares(first, second):
    total = first + second
    positive = total > 0
    inverse = reciprocal(jnp.where(positive, total, 1.0))
    return first * inverse, second * inverse, positive


def window_kernel(cols, width, path, got, out, temps, keffs, rates, gains, kap, acts, lam, mu, kgrad, heat, hcoef, hgrad):
    planes = got.shape[0]
    rows = temps.shape[2]
    half = rows // 2
    steps = path.shape[0]
    spots = path.shape[1]
    base = lax.axis_index("gx") * width
    lane = lane_iota(rows)
    depth = lax.broadcasted_iota(jnp.int32, (rows, LANES), 0)
    inner = depth < rows - 1
    top_row = lax.broadcasted_iota(jnp.int32, (8, LANES), 0) == 0

    lane_p = lane_iota(planes)
    col = base + jnp.where(lane_p < LEFT, lane_p, lane_p - LANES)
    cell = lax.broadcasted_iota(jnp.int32, (planes, LANES), 0) * cols + col
    cell = jnp.where((col >= 0) & (col < cols), cell, -1)
    for n in range(steps):
        count = jnp.zeros((planes, LANES), jnp.float32)
        for s in range(spots):
            count = count + jnp.where(cell == path[n, s], 1.0, 0.0)
        heat[n] = POWER * count

    column = base + jnp.where(lane < LEFT, lane, lane - LANES)
    inside = (column >= 0) & (column < cols)

    def active(act, n):
        return jnp.where(act <= n, 1.0, 0.1)

    def unpack(p, carry):
        a = got[p, 0:rows]
        b = got[p, rows : 2 * rows]
        c = got[p, 2 * rows : 2 * rows + half]
        temps[0, p] = a
        k = jnp.where(inside, b, 0.0)
        kap[p] = k
        act = jnp.where((lane < 25) | (lane >= 121), pltpu.roll(a, LANES - 96, axis=1), pltpu.roll(b, LANES - 50, axis=1))
        acts[p] = act
        cot = jnp.concatenate([c, pltpu.roll(c, HALF, axis=1)], axis=0)
        cot = jnp.where(
            lane < HALF,
            cot,
            jnp.where(lane < LEFT, pltpu.roll(a, LANES - 11, axis=1), pltpu.roll(a, LANES - 75, axis=1)),
        )
        lam[p] = cot
        keffs[0, p] = k * active(act, 0.0) * (1.0 + 0.5 * a)
        return carry

    lax.fori_loop(0, planes, unpack, 0)
    zero = jnp.zeros((rows, LANES), jnp.float32)
    for n in range(steps):
        temps[n, planes] = zero
        keffs[n, planes] = zero
    mu[planes] = zero

    def forward(n):
        def step(p, behind):
            t = temps[n, p]
            a = keffs[n, p]

            def flow(b, dt):
                total = a + b
                return a * b * reciprocal(jnp.where(total > 0, total, 1.0)) * dt

            fx = flow(keffs[n, p + 1], temps[n, p + 1] - t)
            fy = flow(pltpu.roll(a, LANES - 1, axis=1), pltpu.roll(t, LANES - 1, axis=1) - t)
            fz = flow(pltpu.roll(a, rows - 1, axis=0), jnp.where(inner, pltpu.roll(t, rows - 1, axis=0) - t, 0.0))
            flux = 2.0 * ((fx - behind) + (fy - pltpu.roll(fy, 1, axis=1)) + (fz - pltpu.roll(fz, 1, axis=0)))
            shifted = t - MELT
            bump = LATENT * jnp.exp2(jnp.square(shifted) * (-1.0 / (SPREAD * SPREAD * math.log(2.0))))
            inv_c = reciprocal(1.0 + bump)
            rate = DELTA * inv_c
            t8 = t[0:8]
            h = got[p, 2 * rows + half : 2 * rows + half + 1]
            code = got[p, 2 * rows + half + 1 : 2 * rows + half + 2]
            square = t8 * t8
            radiative = code == 1.0
            linear = t8 - jnp.where(code == 0.0, AMBIENT, SUBSTRATE)
            shape = jnp.where(radiative, EMISSION * (square * square - AMBIENT**4), linear)
            slope = jnp.where(radiative, 4.0 * EMISSION * square * t8, 1.0)
            surface = jnp.where(top_row, heat[n, pl.ds(p, 1)] - h * shape, 0.0)
            flux = jnp.concatenate([flux[0:8] + surface, flux[8:]], axis=0)
            dt = flux * rate
            gain = 1.0 + dt * (bump * inv_c) * (shifted * (2.0 / (SPREAD * SPREAD)))
            gain = jnp.concatenate([gain[0:8] - jnp.where(top_row, rate[0:8] * h * slope, 0.0), gain[8:]], axis=0)
            gains[n, p] = gain
            hcoef[n, pl.ds(p, 1)] = -(rate[0:8] * shape)[0:1]
            if n < steps - 1:
                rates[n, p] = rate
                after = t + dt
                temps[n + 1, p] = after
                keffs[n + 1, p] = kap[p] * active(acts[p], float(n + 1)) * (1.0 + 0.5 * after)
            else:
                mu[p] = lam[p] * rate
            return fx

        lax.fori_loop(0, planes, step, zero)

    for n in range(steps):
        forward(n)

    def backward(n):
        def step(p, carry):
            behind_e, behind_p = carry
            t = temps[n, p]
            a = keffs[n, p]
            m = mu[p]

            def adjoint(b, dt, dm):
                ra, rb, positive = shares(a, b)
                q = dt * dm
                energy = a * rb * dm
                return energy, rb * jnp.where(positive, rb, 1.0) * q, ra * jnp.where(positive, ra, 1.0) * q

            ex, px, qx = adjoint(keffs[n, p + 1], temps[n, p + 1] - t, mu[p + 1] - m)
            ey, py, qy = adjoint(
                pltpu.roll(a, LANES - 1, axis=1), pltpu.roll(t, LANES - 1, axis=1) - t, pltpu.roll(m, LANES - 1, axis=1) - m
            )
            ez, pz, qz = adjoint(
                pltpu.roll(a, rows - 1, axis=0),
                pltpu.roll(t, rows - 1, axis=0) - t,
                jnp.where(inner, pltpu.roll(m, rows - 1, axis=0) - m, 0.0),
            )
            energy = (ex - behind_e) + (ey - pltpu.roll(ey, 1, axis=1)) + (ez - pltpu.roll(ez, 1, axis=0))
            pull = (px + behind_p) + (py + pltpu.roll(qy, 1, axis=1)) + (pz + pltpu.roll(qz, 1, axis=0))
            on = active(acts[p], float(n))
            old = lam[p]
            new = old * gains[n, p] + 2.0 * energy - pull * (kap[p] * on)
            grad = pull * (on * (2.0 + t))
            hg = old[0:1] * hcoef[n, pl.ds(p, 1)]
            if n < steps - 1:
                grad = kgrad[p] + grad
                hg = hgrad[pl.ds(p, 1)] + hg
            if n > 0:
                lam[p] = new
                mu[p] = new * rates[n - 1, p]
                kgrad[p] = grad
                hgrad[pl.ds(p, 1)] = hg
            else:
                out[p, 0:rows] = jnp.where(lane < HALF, new, pltpu.roll(-grad, HALF, axis=1))
                out[p, rows : rows + 8] = jnp.broadcast_to(hg, (8, LANES))
            return ex, qx

        lax.fori_loop(0, planes, step, (zero, zero))

    for n in reversed(range(steps)):
        backward(n)


def unpack_kernel(width, got, adjoint, kgrad, hgrad):
    rows = adjoint.shape[1]
    per_tile = LANES // width
    lane = lane_iota(rows)
    for tile in range(adjoint.shape[2] // LANES):
        adj = grad = face = None
        for i in range(per_tile):
            part = got[tile * per_tile + i, 0:rows]
            other = pltpu.roll(part, (i * width + HALF) % LANES, axis=1)
            hface = got[tile * per_tile + i, rows : rows + 1]
            if i:
                part = pltpu.roll(part, i * width, axis=1)
                hface = pltpu.roll(hface, i * width, axis=1)
                adj = jnp.where(lane < i * width, adj, part)
                grad = jnp.where(lane < i * width, grad, other)
                face = jnp.where(lane[0:1] < i * width, face, hface)
            else:
                adj, grad, face = part, other, hface
        place = slice(tile * LANES, (tile + 1) * LANES)
        adjoint[0, :, place] = adj
        kgrad[0, :, place] = grad
        hgrad[:, place] = face


def body(temp0, kappa, act_step, hface, codes, path, cotangent):
    parts = lax.axis_size("gx")
    cols = temp0.shape[2]
    rows = temp0.shape[1]
    width = cols // parts
    planes = parts * temp0.shape[0]
    steps = path.shape[0]
    vmem = pl.BlockSpec(memory_space=pltpu.VMEM)
    smem = pl.BlockSpec(memory_space=pltpu.SMEM)
    params = pltpu.CompilerParams(vmem_limit_bytes=56 * 1024 * 1024)

    def pack(*refs):
        pack_kernel(parts, width, *refs)

    packed = pl.pallas_call(
        pack,
        out_shape=jax.ShapeDtypeStruct((parts, IN_ROWS, LANES), jnp.float32),
        in_specs=[vmem] * 6,
        out_specs=vmem,
        compiler_params=params,
    )(temp0, kappa, act_step, hface, codes, cotangent)
    got = lax.all_to_all(packed, "gx", 0, 0, tiled=True)

    def compute(*refs):
        window_kernel(cols, width, *refs)

    cube = (rows, LANES)
    result = pl.pallas_call(
        compute,
        out_shape=jax.ShapeDtypeStruct((planes, OUT_ROWS, LANES), jnp.float32),
        in_specs=[smem, vmem],
        out_specs=vmem,
        scratch_shapes=[
            pltpu.VMEM((steps, planes + 1) + cube, jnp.float32),
            pltpu.VMEM((steps, planes + 1) + cube, jnp.float32),
            pltpu.VMEM((steps - 1, planes) + cube, jnp.float32),
            pltpu.VMEM((steps, planes) + cube, jnp.float32),
            pltpu.VMEM((planes,) + cube, jnp.float32),
            pltpu.VMEM((planes,) + cube, jnp.float32),
            pltpu.VMEM((planes,) + cube, jnp.float32),
            pltpu.VMEM((planes + 1,) + cube, jnp.float32),
            pltpu.VMEM((planes,) + cube, jnp.float32),
            pltpu.VMEM((steps, planes, LANES), jnp.float32),
            pltpu.VMEM((steps, planes, LANES), jnp.float32),
            pltpu.VMEM((planes, LANES), jnp.float32),
        ],
        compiler_params=params,
    )(path, got)
    back = lax.all_to_all(result, "gx", 0, 0, tiled=True)

    def unpack(*refs):
        unpack_kernel(width, *refs)

    return pl.pallas_call(
        unpack,
        out_shape=(
            jax.ShapeDtypeStruct(temp0.shape, jnp.float32),
            jax.ShapeDtypeStruct(kappa.shape, jnp.float32),
            jax.ShapeDtypeStruct(hface.shape, jnp.float32),
        ),
        in_specs=[vmem],
        out_specs=(vmem, vmem, vmem),
        compiler_params=params,
    )(back)


def solution(mesh):
    placed = (
        P(("groups", "gx"), None, None),
        P(("groups", "gx"), None, None),
        P(("groups", "gx"), None, None),
        P(("groups", "gx"), None),
        P(("groups", "gx"), None),
        P("groups", None),
        P(("groups", "gx"), None, None),
    )
    return jax.shard_map(
        body,
        mesh=mesh,
        in_specs=placed,
        out_specs=(
            P(("groups", "gx"), None, None),
            P(("groups", "gx"), None, None),
            P(("groups", "gx"), None),
        ),
        check_vma=False,
    )
```

time: 104 us -> 73.1 us (0.70)
  the two profiles are of different devices: /device:TPU:3 before, /device:TPU:0 now
where the time goes in v1:
time: 73.1 us; the launch traced here: 72.7 us
  blocking collectives  41.9 us (57%)
  Pallas kernels  30.2 us (41%)
    all_to_all x1, blocking collectives, body(): got = lax.all_to_all(packed, 'gx', 0, 0, tiled=True)  26.6 us
    pallas_call x1, Pallas kernels, body(): pl.pallas_call(compute, out_shape=jax.ShapeDtypeStruct((planes, OUT_ROWS,...  25.3 us
    all_to_all x1, blocking collectives, body(): back = lax.all_to_all(result, 'gx', 0, 0, tiled=True)  15.3 us
    pallas_call x1, Pallas kernels, body(): pl.pallas_call(pack, out_shape=jax.ShapeDtypeStruct((parts, IN_ROWS, LANE...  3.1 us
    pallas_call x1, Pallas kernels, body(): pl.pallas_call(unpack, out_shape=(jax.ShapeDtypeStruct(temp0.shape, jnp.f...  1.79 us

profile of v1, /device:TPU:0, one launch (start us, length us, event | category | flops | bytes accessed | tf_op | source)
XLA Modules:
  0.0 72.7 jit_solution(11958574114360794667)
XLA Ops:
  0.6 3.1 %shard_map.94 = f32[16,88,128]{2,1,0:T(8,128)} custom-call(f32[1,32,1024]{2,1,0:T(8,128)} %refs_0_.2, f32[1,32,1024]{2,1,0:T(8,128)} %refs_1_.1, s32[1,32,1024]{2,1,0:T(8,128)} %refs_2_.1, f32[1,1024]{1,0:T(1,128)} %refs_3_.1, s32[1,1024]{1,0:T(1,128)} %refs_4_.1, f32[1,32,1024]{2,1,0:T(8,128)} %refs_5_.1), custom_call_target="tpu_custom_call" | custom-call | tf_op jit(solution)/shard_map/pallas_call | solution.py:272
  3.7 26.6 %all_to_all.10.refs_1_ = f32[16,88,128]{2,1,0:T(8,128)} all-to-all(f32[16,88,128]{2,1,0:T(8,128)} %shard_map.94), channel_id=1, replica_groups=mesh['groups'=2,'gx'=16] {'gx'}, dimensions={0} | all-to-all | bytes 1441792 | tf_op jit(solution)/shard_map/all_to_all | solution.py:279
  30.3 25.3 %shard_map.95 = f32[16,40,128]{2,1,0:T(8,128)} custom-call(s32[4,32]{1,0:T(4,128)} %refs_0_.3, f32[16,88,128]{2,1,0:T(8,128)} %all_to_all.10.refs_1_), custom_call_target="tpu_custom_call" | custom-call | tf_op jit(solution)/shard_map/pallas_call | solution.py:285
  55.6 15.3 %all_to_all.11.refs_0_ = f32[16,40,128]{2,1,0:T(8,128)} all-to-all(f32[16,40,128]{2,1,0:T(8,128)} %shard_map.95), channel_id=1, replica_groups=mesh['groups'=2,'gx'=16] {'gx'}, dimensions={0} | all-to-all | bytes 655360 | tf_op jit(solution)/shard_map/all_to_all | solution.py:306
  70.9 1.8 %shard_map.96 = (f32[1,32,1024]{2,1,0:T(8,128)}, f32[1,32,1024]{2,1,0:T(8,128)}, f32[1,1024]{1,0:T(1,128)}) custom-call(f32[16,40,128]{2,1,0:T(8,128)} %all_to_all.11.refs_0_), custom_call_target="tpu_custom_call" | custom-call | tf_op jit(solution)/shard_map/pallas_call | solution.py:311

commit v2 on v1

--- a/solution.py
+++ b/solution.py
@@ -21,13 +21,24 @@
 LEFT = 96
 IN_ROWS = 88
 OUT_ROWS = 40
+UNROLL = 8
+MIB = 1024 * 1024
 
 
 def lane_iota(rows):
     return lax.broadcasted_iota(jnp.int32, (rows, LANES), 1)
 
 
-def pack_kernel(parts, width, temp, kappa, act, hface, codes, cot, out):
+def pack_kernel(parts, width, *refs):
+    sources, out, (temp, kappa, act, hface, codes, cot), done = refs[:6], refs[6], refs[7:13], refs[13]
+    copies = [
+        pltpu.make_async_copy(source, held, done.at[i])
+        for i, (source, held) in enumerate(zip(sources, (temp, kappa, act, hface, codes, cot)))
+    ]
+    for copy in copies:
+        copy.start()
+    for copy in copies:
+        copy.wait()
     tiles = temp.shape[-1] // LANES
 
     def window(ref, start, rows):
@@ -130,7 +141,7 @@
         keffs[0, p] = k * active(act, 0.0) * (1.0 + 0.5 * a)
         return carry
 
-    lax.fori_loop(0, planes, unpack, 0)
+    lax.fori_loop(0, planes, unpack, 0, unroll=UNROLL)
     zero = jnp.zeros((rows, LANES), jnp.float32)
     for n in range(steps):
         temps[n, planes] = zero
@@ -178,7 +189,7 @@
                 mu[p] = lam[p] * rate
             return fx
 
-        lax.fori_loop(0, planes, step, zero)
+        lax.fori_loop(0, planes, step, zero, unroll=UNROLL)
 
     for n in range(steps):
         forward(n)
@@ -225,7 +236,7 @@
                 out[p, rows : rows + 8] = jnp.broadcast_to(hg, (8, LANES))
             return ex, qx
 
-        lax.fori_loop(0, planes, step, (zero, zero))
+        lax.fori_loop(0, planes, step, (zero, zero), unroll=UNROLL)
 
     for n in reversed(range(steps)):
         backward(n)
@@ -264,7 +275,11 @@
     steps = path.shape[0]
     vmem = pl.BlockSpec(memory_space=pltpu.VMEM)
     smem = pl.BlockSpec(memory_space=pltpu.SMEM)
-    params = pltpu.CompilerParams(vmem_limit_bytes=56 * 1024 * 1024)
+
+    def params(words):
+        return pltpu.CompilerParams(vmem_limit_bytes=4 * words + 2 * MIB)
+
+    plane = rows * LANES
 
     def pack(*refs):
         pack_kernel(parts, width, *refs)
@@ -272,10 +287,12 @@
     packed = pl.pallas_call(
         pack,
         out_shape=jax.ShapeDtypeStruct((parts, IN_ROWS, LANES), jnp.float32),
-        in_specs=[vmem] * 6,
+        in_specs=[pl.BlockSpec(memory_space=pltpu.HBM)] * 6,
         out_specs=vmem,
-        compiler_params=params,
-    )(temp0, kappa, act_step, hface, codes, cotangent)
+        scratch_shapes=[pltpu.VMEM(x.shape, x.dtype) for x in (temp0, kappa, act_step, hface, codes, cotangent)]
+        + [pltpu.SemaphoreType.DMA((6,))],
+        compiler_params=params(4 * rows * cols + parts * IN_ROWS * LANES),
+    )(*[pltpu.with_memory_space_constraint(x, pltpu.HBM) for x in (temp0, kappa, act_step, hface, codes, cotangent)])
     got = lax.all_to_all(packed, "gx", 0, 0, tiled=True)
 
     def compute(*refs):
@@ -301,7 +318,7 @@
             pltpu.VMEM((steps, planes, LANES), jnp.float32),
             pltpu.VMEM((planes, LANES), jnp.float32),
         ],
-        compiler_params=params,
+        compiler_params=params(planes * (24 * plane + (IN_ROWS + OUT_ROWS) * LANES)),
     )(path, got)
     back = lax.all_to_all(result, "gx", 0, 0, tiled=True)
 
@@ -317,7 +334,7 @@
         ),
         in_specs=[vmem],
         out_specs=(vmem, vmem, vmem),
-        compiler_params=params,
+        compiler_params=params(2 * rows * cols + planes * OUT_ROWS * LANES),
     )(back)
 
 

time: 73.1 us -> 52.5 us (0.72)
  Pallas kernels: 30.2 us -> 10.8 us
  blocking collectives: 41.9 us -> 40.8 us
    pallas_call x1, Pallas kernels: 25.3 us -> 7.72 us  [body(): pl.pallas_call(compute, out_shape=jax.ShapeDtypeStruct((planes, OUT_ROWS,...]
    pallas_call x1, Pallas kernels: 1.79 us -> 0.82 us  [body(): pl.pallas_call(unpack, out_shape=(jax.ShapeDtypeStruct(temp0.shape, jnp.f...]
    pallas_call x1, Pallas kernels: 3.1 us -> 2.29 us  [body(): pl.pallas_call(pack, out_shape=jax.ShapeDtypeStruct((parts, IN_ROWS, LANE...]
    all_to_all x1, blocking collectives: 15.3 us -> 14.5 us  [body(): back = lax.all_to_all(result, 'gx', 0, 0, tiled=True)]
where the time goes in v2:
time: 52.5 us; the launch traced here: 52.3 us
  blocking collectives  40.8 us (78%)
  Pallas kernels  10.8 us (21%)
  between operations  0.65 us (1%)
    all_to_all x1, blocking collectives, body(): got = lax.all_to_all(packed, 'gx', 0, 0, tiled=True)  26.3 us
    all_to_all x1, blocking collectives, body(): back = lax.all_to_all(result, 'gx', 0, 0, tiled=True)  14.5 us
    pallas_call x1, Pallas kernels, body(): pl.pallas_call(compute, out_shape=jax.ShapeDtypeStruct((planes, OUT_ROWS,...  7.72 us
    pallas_call x1, Pallas kernels, body(): pl.pallas_call(pack, out_shape=jax.ShapeDtypeStruct((parts, IN_ROWS, LANE...  2.29 us

profile of v2, /device:TPU:0, one launch (start us, length us, event | category | flops | bytes accessed | tf_op | source)
XLA Modules:
  0.0 52.3 jit_solution(15339847185251281902)
XLA Ops:
  0.6 2.3 %shard_map.94 = f32[16,88,128]{2,1,0:T(8,128)S(1)} custom-call(f32[1,32,1024]{2,1,0:T(8,128)} %refs_0_.2, f32[1,32,1024]{2,1,0:T(8,128)} %refs_1_.1, s32[1,32,1024]{2,1,0:T(8,128)} %refs_2_.1, f32[1,1024]{1,0:T(1,128)} %refs_3_.1, s32[1,1024]{1,0:T(1,128)} %refs_4_.1, f32[1,32,1024]{2,1,0:T(8,128)} %refs_5_.1), custom_call_target="tpu_custom_call" | custom-call | tf_op jit(solution)/shard_map/pallas_call | solution.py:287
  2.9 0.0 copy-start
  2.9 26.3 %all_to_all.10.refs_1_ = f32[16,88,128]{2,1,0:T(8,128)S(1)} all-to-all(f32[16,88,128]{2,1,0:T(8,128)S(1)} %shard_map.94), channel_id=1, replica_groups=mesh['groups'=2,'gx'=16] {'gx'}, dimensions={0} | all-to-all | bytes 1441792 | tf_op jit(solution)/shard_map/all_to_all | solution.py:296
  29.2 0.0 copy-done
  29.2 7.7 %shard_map.95 = f32[16,40,128]{2,1,0:T(8,128)S(1)} custom-call(s32[4,32]{1,0:T(4,128)S(1)} %copy-done, f32[16,88,128]{2,1,0:T(8,128)S(1)} %all_to_all.10.refs_1_), custom_call_target="tpu_custom_call" | custom-call | tf_op jit(solution)/shard_map/pallas_call | solution.py:302
  36.9 14.5 %all_to_all.11.refs_0_ = f32[16,40,128]{2,1,0:T(8,128)S(1)} all-to-all(f32[16,40,128]{2,1,0:T(8,128)S(1)} %shard_map.95), channel_id=1, replica_groups=mesh['groups'=2,'gx'=16] {'gx'}, dimensions={0} | all-to-all | bytes 655360 | tf_op jit(solution)/shard_map/all_to_all | solution.py:323
  51.5 0.8 %shard_map.96 = (f32[1,32,1024]{2,1,0:T(8,128)}, f32[1,32,1024]{2,1,0:T(8,128)}, f32[1,1024]{1,0:T(1,128)}) custom-call(f32[16,40,128]{2,1,0:T(8,128)S(1)} %all_to_all.11.refs_0_), custom_call_target="tpu_custom_call" | custom-call | tf_op jit(solution)/shard_map/pallas_call | solution.py:328
Async XLA Ops:
  2.9 26.3 %copy-start = (s32[4,32]{1,0:T(4,128)S(1)}, s32[4,32]{1,0:T(4,128)}, u32[]{:S(2)}) copy-start(s32[4,32]{1,0:T(4,128)} %refs_0_.3) | copy-start | bytes 1540

commit v3 on v2

v3 whole, which is shorter than its diff:
```python
import math

import jax
import jax.numpy as jnp
from jax import lax
from jax.experimental import pallas as pl
from jax.experimental.pallas import tpu as pltpu
from jax.sharding import PartitionSpec as P

LATENT = 1.5
MELT = 1.0
SPREAD = 0.15
DELTA = 0.05
EMISSION = 0.1
POWER = 8.0
AMBIENT = 0.2
SUBSTRATE = 0.5

LANES = 128
HALF = 64
LEFT = 96
UNROLL = 8
MIB = 1024 * 1024


def lane_iota(rows):
    return lax.broadcasted_iota(jnp.int32, (rows, LANES), 1)


ACT_LOW, ACT_HIGH, COT_RIGHT, COT_LEFT, FACE = 96, 50, 11, 75, 79


def in_rows(rows):
    return 2 * rows + rows // 2


def out_rows(rows):
    return rows + 1


def pack_kernel(parts, width, *refs):
    path, *sources = refs[:7]
    out, heat = refs[7:9]
    spots, temp, kappa, act, hface, codes, cot, faces, done = refs[9:]
    cols = temp.shape[-1]
    rows = temp.shape[1]
    half = rows // 2
    tiles = cols // LANES
    copies = [
        pltpu.make_async_copy(source, held, done.at[i])
        for i, (source, held) in enumerate(zip([path] + sources, (spots, temp, kappa, act, hface, codes, cot)))
    ]
    for copy in copies:
        copy.start()

    planes = heat.shape[1]
    base = lax.axis_index("gx") * width
    place = (lane_iota(planes) - lax.rem(base, LANES)) & (LANES - 1)
    col = base + jnp.where(place < LEFT, place, place - LANES)
    cell = lax.broadcasted_iota(jnp.int32, (planes, LANES), 0) * cols + col
    cell = jnp.where((col >= 0) & (col < cols), cell, -1)
    copies[0].wait()
    for n in range(heat.shape[0]):
        count = jnp.zeros((planes, LANES), jnp.float32)
        for s in range(spots.shape[1]):
            count = count + jnp.where(cell == spots[n, s], 1.0, 0.0)
        heat[n] = POWER * count

    for copy in copies[1:]:
        copy.wait()
    faces[0:8] = jnp.broadcast_to(hface[...], (8, cols))
    faces[8:16] = jnp.broadcast_to(codes[...].astype(jnp.float32), (8, cols))

    lane_of = lane_iota(rows)
    for d in range(parts):
        tile, off = divmod(d * width, LANES)
        lane = (lane_of - off) & (LANES - 1)

        def window(ref):
            def part(t):
                place = slice(min(max(t, 0), tiles - 1) * LANES, (min(max(t, 0), tiles - 1) + 1) * LANES)
                value = ref[0, :, place] if len(ref.shape) == 3 else ref[:, place]
                return value.astype(jnp.float32)

            count = ref.shape[-2]
            result = part(tile)
            if off > LANES - HALF - 7:
                result = jnp.where((lane_of[:count] < off) & (lane[:count] < LEFT), part(tile + 1), result)
            if off < 7:
                result = jnp.where((lane_of[:count] >= off) & (lane[:count] >= LEFT), part(tile - 1), result)
            return result

        t = window(temp)
        k = window(kappa)
        a = window(act)
        c = window(cot)
        face = window(faces)
        extra = jnp.where(
            lane >= 89,
            pltpu.roll(a, ACT_LOW, axis=1),
            jnp.where(lane >= 75, pltpu.roll(c, COT_RIGHT, axis=1), pltpu.roll(c, COT_LEFT, axis=1)),
        )
        face = jnp.concatenate(
            [pltpu.roll(x, FACE + 7 - 70, axis=1, stride=10, stride_axis=0) for x in (face[0:8], face[8:16])], axis=0
        )
        face = jnp.where((lane[:16] >= FACE) & (lane[:16] < 89), face, extra[:16])
        extra = jnp.concatenate([face, extra[16:]], axis=0)
        out[d, 0:rows] = jnp.where((lane >= 71) & (lane < 121), extra, t)
        out[d, rows : 2 * rows] = jnp.where((lane >= 75) & (lane < 121), pltpu.roll(a, ACT_HIGH, axis=1), k)
        out[d, 2 * rows : 2 * rows + half] = jnp.where(
            lane[:half] < HALF, c[:half], pltpu.roll(c[half:], HALF, axis=1)
        )


def reciprocal(value):
    return 1.0 / value


def shares(first, second):
    total = first + second
    positive = total > 0
    inverse = reciprocal(jnp.where(positive, total, 1.0))
    return first * inverse, second * inverse, positive


def window_kernel(
    cols, width, got, heat, out, temps, keffs, rates, gains, kap, acts, lam, mu, kgrad, hcoef, hgrad, hrow, crow, *faces
):
    steps, planes = heat.shape[:2]
    rows = temps.shape[2]
    half = rows // 2
    base = lax.axis_index("gx") * width
    lane = (lane_iota(rows) - lax.rem(base, LANES)) & (LANES - 1)
    depth = lax.broadcasted_iota(jnp.int32, (rows, LANES), 0)
    inner = depth < rows - 1
    top_row = lax.broadcasted_iota(jnp.int32, (8, LANES), 0) == 0
    column = base + jnp.where(lane < LEFT, lane, lane - LANES)
    inside = (column >= 0) & (column < cols)

    place = jnp.where(lane[:8] < LEFT, lane[:8], lane[:8] - LANES) + 7 - 10 * (7 - depth[:8])
    face_mask = (place >= 0) & (place < 10)

    def active(act, n):
        return jnp.where(act <= n, 1.0, 0.1)

    def unpack(p, carry):
        a = got[p, 0:rows]
        b = got[p, rows : 2 * rows]
        c = got[p, 2 * rows : 2 * rows + half]
        temps[0, p] = a
        k = jnp.where(inside, b, 0.0)
        kap[p] = k
        act = jnp.where(
            (lane < 25) | (lane >= 121),
            pltpu.roll(a, LANES - ACT_LOW, axis=1),
            pltpu.roll(b, LANES - ACT_HIGH, axis=1),
        )
        acts[p] = act
        cot = jnp.concatenate([c, pltpu.roll(c, HALF, axis=1)], axis=0)
        cot = jnp.where(
            lane < HALF,
            cot,
            jnp.where(lane < LEFT, pltpu.roll(a, LANES - COT_RIGHT, axis=1), pltpu.roll(a, LANES - COT_LEFT, axis=1)),
        )
        lam[p] = cot
        face = pltpu.roll(a[0:16], 112, axis=1)
        for bit in (1, 2, 4):
            face = jnp.where((depth[:16] & bit) > 0, pltpu.roll(face, LANES - 10 * bit, axis=1), face)
        hrow[pl.ds(p, 1)] = jnp.sum(jnp.where(face_mask, face[0:8], 0.0), axis=0, keepdims=True)
        crow[pl.ds(p, 1)] = jnp.sum(jnp.where(face_mask, face[8:16], 0.0), axis=0, keepdims=True)
        keffs[0, p] = k * active(act, 0.0) * (1.0 + 0.5 * a)
        return carry

    lax.fori_loop(0, planes, unpack, 0, unroll=UNROLL)
    zero = jnp.zeros((rows, LANES), jnp.float32)
    for n in range(steps):
        temps[n, planes] = zero
        keffs[n, planes] = zero
    mu[planes] = zero

    def forward(n):
        def step(p, behind):
            t = temps[n, p]
            a = keffs[n, p]

            def flow(axis, b, dt):
                first, second, positive = shares(a, b)
                half_g = a * second
                if faces:
                    faces[0][n, axis, p] = half_g
                    faces[0][n, axis + 1, p] = second * jnp.where(positive, second, 1.0) * dt
                    faces[0][n, axis + 2, p] = first * jnp.where(positive, first, 1.0) * dt
                return half_g * dt

            fx = flow(0, keffs[n, p + 1], temps[n, p + 1] - t)
            fy = flow(3, pltpu.roll(a, LANES - 1, axis=1), pltpu.roll(t, LANES - 1, axis=1) - t)
            fz = flow(6, pltpu.roll(a, rows - 1, axis=0), jnp.where(inner, pltpu.roll(t, rows - 1, axis=0) - t, 0.0))
            flux = 2.0 * ((fx - behind) + (fy - pltpu.roll(fy, 1, axis=1)) + (fz - pltpu.roll(fz, 1, axis=0)))
            shifted = t - MELT
            bump = LATENT * jnp.exp2(jnp.square(shifted) * (-1.0 / (SPREAD * SPREAD * math.log(2.0))))
            inv_c = reciprocal(1.0 + bump)
            rate = DELTA * inv_c
            t8 = t[0:8]
            h = hrow[pl.ds(p, 1)]
            code = crow[pl.ds(p, 1)]
            square = t8 * t8
            radiative = code == 1.0
            linear = t8 - jnp.where(code == 0.0, AMBIENT, SUBSTRATE)
            shape = jnp.where(radiative, EMISSION * (square * square - AMBIENT**4), linear)
            slope = jnp.where(radiative, 4.0 * EMISSION * square * t8, 1.0)
            surface = jnp.where(top_row, heat[n, pl.ds(p, 1)] - h * shape, 0.0)
            flux = jnp.concatenate([flux[0:8] + surface, flux[8:]], axis=0)
            dt = flux * rate
            gain = 1.0 + dt * (bump * inv_c) * (shifted * (2.0 / (SPREAD * SPREAD)))
            gain = jnp.concatenate([gain[0:8] - jnp.where(top_row, rate[0:8] * h * slope, 0.0), gain[8:]], axis=0)
            gains[n, p] = gain
            hcoef[n, pl.ds(p, 1)] = -(rate[0:8] * shape)[0:1]
            if n < steps - 1:
                rates[n, p] = rate
                after = t + dt
                temps[n + 1, p] = after
                keffs[n + 1, p] = kap[p] * active(acts[p], float(n + 1)) * (1.0 + 0.5 * after)
            else:
                mu[p] = lam[p] * rate
            return fx

        lax.fori_loop(0, planes, step, zero, unroll=UNROLL)

    for n in range(steps):
        forward(n)

    def backward(n):
        def step(p, carry, store=None):
            behind_e, behind_p = carry
            t = temps[n, p]
            m = mu[p]

            def adjoint(axis, dm, ends):
                if faces:
                    half_g, first, second = (faces[0][n, axis + i, p] for i in range(3))
                    return half_g * dm, first * dm, second * dm
                a = keffs[n, p]
                b, dt = ends(a)
                first, second, positive = shares(a, b)
                q = dt * dm
                return (
                    a * second * dm,
                    second * jnp.where(positive, second, 1.0) * q,
                    first * jnp.where(positive, first, 1.0) * q,
                )

            def rolled(axis, count):
                return lambda a: (pltpu.roll(a, count - 1, axis=axis), pltpu.roll(t, count - 1, axis=axis) - t)

            ex, px, qx = adjoint(0, mu[p + 1] - m, lambda a: (keffs[n, p + 1], temps[n, p + 1] - t))
            ey, py, qy = adjoint(3, pltpu.roll(m, LANES - 1, axis=1) - m, rolled(1, LANES))
            ez, pz, qz = adjoint(6, jnp.where(inner, pltpu.roll(m, rows - 1, axis=0) - m, 0.0), rolled(0, rows))
            energy = (ex - behind_e) + (ey - pltpu.roll(ey, 1, axis=1)) + (ez - pltpu.roll(ez, 1, axis=0))
            pull = (px + behind_p) + (py + pltpu.roll(qy, 1, axis=1)) + (pz + pltpu.roll(qz, 1, axis=0))
            on = active(acts[p], float(n))
            old = lam[p]
            new = old * gains[n, p] + 2.0 * energy - pull * (kap[p] * on)
            grad = pull * (on * (2.0 + t))
            hg = old[0:1] * hcoef[n, pl.ds(p, 1)]
            if n < steps - 1:
                grad = kgrad[p] + grad
                hg = hgrad[pl.ds(p, 1)] + hg
            if n > 0:
                lam[p] = new
                mu[p] = new * rates[n - 1, p]
                kgrad[p] = grad
                hgrad[pl.ds(p, 1)] = hg
            else:
                store(jnp.where(lane < HALF, new, pltpu.roll(-grad, HALF, axis=1)), hg)
            return ex, qx

        def last(i, carry):
            size = UNROLL * out_rows(rows)
            chunk = out.at[pl.ds(pl.multiple_of(i * size, 8), size)]
            for j in range(UNROLL):

                def store(cube, row, at=j * out_rows(rows)):
                    chunk[at : at + rows] = cube
                    chunk[at + rows : at + rows + 1] = row

                carry = step(i * UNROLL + j, carry, store)
            return carry

        if n > 0:
            lax.fori_loop(0, planes, step, (zero, zero), unroll=UNROLL)
        else:
            lax.fori_loop(0, planes // UNROLL, last, (zero, zero))

    for n in reversed(range(steps)):
        backward(n)


def unpack_kernel(width, got, adjoint, kgrad, hgrad):
    rows = adjoint.shape[1]
    per_tile = LANES // width
    lane = lane_iota(rows)
    turned = (lane - HALF) & (LANES - 1)
    for tile in range(adjoint.shape[2] // LANES):
        adj = grad = face = None
        for i in range(per_tile):
            at = (tile * per_tile + i) * out_rows(rows)
            part = got[at : at + rows]
            row = got[at + rows : at + rows + 1]
            adj = part if i == 0 else jnp.where(lane < i * width, adj, part)
            grad = part if i == 0 else jnp.where(turned < i * width, grad, part)
            face = row if i == 0 else jnp.where(lane[0:1] < i * width, face, row)
        place = slice(tile * LANES, (tile + 1) * LANES)
        adjoint[0, :, place] = adj
        kgrad[0, :, place] = pltpu.roll(grad, HALF, axis=1)
        hgrad[:, place] = face


def body(temp0, kappa, act_step, hface, codes, path, cotangent):
    parts = lax.axis_size("gx")
    cols = temp0.shape[2]
    rows = temp0.shape[1]
    width = cols // parts
    planes = parts * temp0.shape[0]
    steps = path.shape[0]
    vmem = pl.BlockSpec(memory_space=pltpu.VMEM)
    hbm = pl.BlockSpec(memory_space=pltpu.HBM)
    plane = rows * LANES

    def params(words):
        return pltpu.CompilerParams(vmem_limit_bytes=4 * words + 2 * MIB)

    def pack(*refs):
        pack_kernel(parts, width, *refs)

    sources = (temp0, kappa, act_step, hface, codes, cotangent)
    packed, heat = pl.pallas_call(
        pack,
        out_shape=(
            jax.ShapeDtypeStruct((parts, in_rows(rows), LANES), jnp.float32),
            jax.ShapeDtypeStruct((steps, planes, LANES), jnp.float32),
        ),
        in_specs=[hbm] * 7,
        out_specs=(vmem, vmem),
        scratch_shapes=[pltpu.SMEM(path.shape, path.dtype)]
        + [pltpu.VMEM(x.shape, x.dtype) for x in sources]
        + [pltpu.VMEM((16, cols), jnp.float32), pltpu.SemaphoreType.DMA((7,))],
        compiler_params=params(5 * rows * cols + parts * (in_rows(rows) + steps) * LANES),
    )(*[pltpu.with_memory_space_constraint(x, pltpu.HBM) for x in (path,) + sources])
    got = lax.all_to_all(packed, "gx", 0, 0, tiled=True)

    def compute(*refs):
        window_kernel(cols, width, *refs)

    keep = 9 * steps if planes <= 32 else 0

    def held(count, extra=0):
        return pltpu.VMEM(count + (planes + extra, rows, LANES), jnp.float32)

    row = pltpu.VMEM((planes, LANES), jnp.float32)
    result = pl.pallas_call(
        compute,
        out_shape=jax.ShapeDtypeStruct((planes * out_rows(rows), LANES), jnp.float32),
        in_specs=[vmem, vmem],
        out_specs=vmem,
        scratch_shapes=[
            held((steps,), 1),
            held((steps,), 1),
            held((steps - 1,)),
            held((steps,)),
            held(()),
            held(()),
            held(()),
            held((), 1),
            held(()),
            pltpu.VMEM((steps, planes, LANES), jnp.float32),
            row,
            row,
            row,
        ]
        + ([held((steps, 9))] if keep else []),
        compiler_params=params(planes * ((24 + keep) * plane + (in_rows(rows) + out_rows(rows)) * LANES)),
    )(got, heat)
    result = result.reshape(planes, out_rows(rows), 1, LANES)
    back = lax.all_to_all(result, "gx", 0, 0, tiled=True).reshape(planes * out_rows(rows), LANES)

    def unpack(*refs):
        unpack_kernel(width, *refs)

    return pl.pallas_call(
        unpack,
        out_shape=(
            jax.ShapeDtypeStruct(temp0.shape, jnp.float32),
            jax.ShapeDtypeStruct(kappa.shape, jnp.float32),
            jax.ShapeDtypeStruct(hface.shape, jnp.float32),
        ),
        in_specs=[vmem],
        out_specs=(vmem, vmem, vmem),
        compiler_params=params(2 * rows * cols + planes * out_rows(rows) * LANES),
    )(back)


def solution(mesh):
    placed = (
        P(("groups", "gx"), None, None),
        P(("groups", "gx"), None, None),
        P(("groups", "gx"), None, None),
        P(("groups", "gx"), None),
        P(("groups", "gx"), None),
        P("groups", None),
        P(("groups", "gx"), None, None),
    )
    return jax.shard_map(
        body,
        mesh=mesh,
        in_specs=placed,
        out_specs=(
            P(("groups", "gx"), None, None),
            P(("groups", "gx"), None, None),
            P(("groups", "gx"), None),
        ),
        check_vma=False,
    )
```

time: 52.5 us -> 48.8 us (0.930)
  blocking collectives: 40.8 us -> 38.6 us
  Pallas kernels: 10.8 us -> 9.33 us
    pallas_call x2, Pallas kernels: 10 us -> 8.57 us  [the longest x1 6.97 us: body(): pl.pallas_call(compute, out_shape=jax.ShapeDtypeStruct((planes * out_rows...]
    all_to_all x1, blocking collectives: 14.5 us -> 13.2 us  [body(): lax.all_to_all(result, 'gx', 0, 0, tiled=True)]
    all_to_all x1, blocking collectives: 26.3 us -> 25.4 us  [body(): got = lax.all_to_all(packed, 'gx', 0, 0, tiled=True)]
where the time goes in v3:
time: 48.8 us; the launch traced here: 48.6 us
  blocking collectives  38.6 us (79%)
  Pallas kernels  9.33 us (19%)
  between operations  0.65 us (1%)
    all_to_all x1, blocking collectives, body(): got = lax.all_to_all(packed, 'gx', 0, 0, tiled=True)  25.4 us
    all_to_all x1, blocking collectives, body(): lax.all_to_all(result, 'gx', 0, 0, tiled=True)  13.2 us
    pallas_call x1, Pallas kernels, body(): pl.pallas_call(compute, out_shape=jax.ShapeDtypeStruct((planes * out_rows...  6.97 us
    pallas_call x1, Pallas kernels, body(): pl.pallas_call(pack, out_shape=(jax.ShapeDtypeStruct((parts, in_rows(rows...  1.59 us

profile of v3, /device:TPU:0, one launch (start us, length us, event | category | flops | bytes accessed | tf_op | source)
XLA Modules:
  0.0 48.6 jit_solution(17132642265122611213)
XLA Ops:
  0.6 1.6 %shard_map.94 = (f32[16,80,128]{2,1,0:T(8,128)S(1)}, f32[4,16,128]{2,1,0:T(8,128)S(1)}) custom-call(s32[4,32]{1,0:T(4,128)} %refs_0_.1, f32[1,32,1024]{2,1,0:T(8,128)} %refs_1_.1, f32[1,32,1024]{2,1,0:T(8,128)} %refs_2_.1, s32[1,32,1024]{2,1,0:T(8,128)} %refs_3_.1, f32[1,1024]{1,0:T(1,128)} %refs_4_.1, s32[1,1024]{1,0:T(1,128)} %refs_5_.1, ...), custom_call_target="tpu_custom_call" | custom-call | tf_op jit(solution)/shard_map/pallas_call | solution.py:336
  2.2 25.4 %all_to_all.10.refs_0_ = f32[16,80,128]{2,1,0:T(8,128)S(1)} all-to-all(f32[16,80,128]{2,1,0:T(8,128)S(1)} %get-tuple-element.5), channel_id=1, replica_groups=mesh['groups'=2,'gx'=16] {'gx'}, dimensions={0} | all-to-all | bytes 1310720 | tf_op jit(solution)/shard_map/all_to_all | solution.py:349
  27.6 7.0 %shard_map.95 = f32[528,128]{1,0:T(8,128)S(1)} custom-call(f32[16,80,128]{2,1,0:T(8,128)S(1)} %all_to_all.10.refs_0_, f32[4,16,128]{2,1,0:T(8,128)S(1)} %get-tuple-element.6.refs_1_), custom_call_target="tpu_custom_call" | custom-call | tf_op jit(solution)/shard_map/pallas_call | solution.py:360
  34.6 13.2 %all_to_all.11 = f32[16,33,1,128]{3,2,1,0:T(1,128)S(1)} all-to-all(f32[16,33,1,128]{3,2,1,0:T(1,128)S(1)} %bitcast.3), channel_id=1, replica_groups=mesh['groups'=2,'gx'=16] {'gx'}, dimensions={0} | all-to-all | bytes 540672 | tf_op jit(solution)/shard_map/all_to_all | solution.py:384
  47.9 0.8 %shard_map.96 = (f32[1,32,1024]{2,1,0:T(8,128)}, f32[1,32,1024]{2,1,0:T(8,128)}, f32[1,1024]{1,0:T(1,128)}) custom-call(f32[528,128]{1,0:T(8,128)S(1)} %bitcast.2), custom_call_target="tpu_custom_call" | custom-call | tf_op jit(solution)/shard_map/pallas_call | solution.py:389

commit v4 on v3

--- a/solution.py
+++ b/solution.py
@@ -64,7 +64,7 @@
         count = jnp.zeros((planes, LANES), jnp.float32)
         for s in range(spots.shape[1]):
             count = count + jnp.where(cell == spots[n, s], 1.0, 0.0)
-        heat[n] = POWER * count
+        heat[n] = (0.5 * POWER) * count
 
     for copy in copies[1:]:
         copy.wait()
@@ -132,13 +132,16 @@
     base = lax.axis_index("gx") * width
     lane = (lane_iota(rows) - lax.rem(base, LANES)) & (LANES - 1)
     depth = lax.broadcasted_iota(jnp.int32, (rows, LANES), 0)
-    inner = depth < rows - 1
+    bottom = lax.broadcasted_iota(jnp.int32, (8, LANES), 0) == 7
     top_row = lax.broadcasted_iota(jnp.int32, (8, LANES), 0) == 0
     column = base + jnp.where(lane < LEFT, lane, lane - LANES)
     inside = (column >= 0) & (column < cols)
 
     place = jnp.where(lane[:8] < LEFT, lane[:8], lane[:8] - LANES) + 7 - 10 * (7 - depth[:8])
     face_mask = (place >= 0) & (place < 10)
+
+    def above_bottom(value):
+        return jnp.concatenate([value[: rows - 8], jnp.where(bottom, 0.0, value[rows - 8 :])], axis=0)
 
     def active(act, n):
         return jnp.where(act <= n, 1.0, 0.1)
@@ -149,6 +152,7 @@
         c = got[p, 2 * rows : 2 * rows + half]
         temps[0, p] = a
         k = jnp.where(inside, b, 0.0)
+        k = 0.5 * k
         kap[p] = k
         act = jnp.where(
             (lane < 25) | (lane >= 121),
@@ -166,9 +170,9 @@
         face = pltpu.roll(a[0:16], 112, axis=1)
         for bit in (1, 2, 4):
             face = jnp.where((depth[:16] & bit) > 0, pltpu.roll(face, LANES - 10 * bit, axis=1), face)
-        hrow[pl.ds(p, 1)] = jnp.sum(jnp.where(face_mask, face[0:8], 0.0), axis=0, keepdims=True)
+        hrow[pl.ds(p, 1)] = 0.5 * jnp.sum(jnp.where(face_mask, face[0:8], 0.0), axis=0, keepdims=True)
         crow[pl.ds(p, 1)] = jnp.sum(jnp.where(face_mask, face[8:16], 0.0), axis=0, keepdims=True)
-        keffs[0, p] = k * active(act, 0.0) * (1.0 + 0.5 * a)
+        keffs[0, p] = k * active(act, 0.0) * (2.0 + a)
         return carry
 
     lax.fori_loop(0, planes, unpack, 0, unroll=UNROLL)
@@ -179,9 +183,12 @@
     mu[planes] = zero
 
     def forward(n):
-        def step(p, behind):
-            t = temps[n, p]
-            a = keffs[n, p]
+        def ahead(p):
+            return temps[n, p], keffs[n, p]
+
+        def step(p, carry):
+            behind, t, a = carry
+            t_ahead, a_ahead = ahead(p + 1)
 
             def flow(axis, b, dt):
                 first, second, positive = shares(a, b)
@@ -192,14 +199,14 @@
                     faces[0][n, axis + 2, p] = first * jnp.where(positive, first, 1.0) * dt
                 return half_g * dt
 
-            fx = flow(0, keffs[n, p + 1], temps[n, p + 1] - t)
+            fx = flow(0, a_ahead, t_ahead - t)
             fy = flow(3, pltpu.roll(a, LANES - 1, axis=1), pltpu.roll(t, LANES - 1, axis=1) - t)
-            fz = flow(6, pltpu.roll(a, rows - 1, axis=0), jnp.where(inner, pltpu.roll(t, rows - 1, axis=0) - t, 0.0))
-            flux = 2.0 * ((fx - behind) + (fy - pltpu.roll(fy, 1, axis=1)) + (fz - pltpu.roll(fz, 1, axis=0)))
+            fz = flow(6, pltpu.roll(a, rows - 1, axis=0), above_bottom(pltpu.roll(t, rows - 1, axis=0) - t))
+            flux = (fx - behind) + (fy - pltpu.roll(fy, 1, axis=1)) + (fz - pltpu.roll(fz, 1, axis=0))
             shifted = t - MELT
             bump = LATENT * jnp.exp2(jnp.square(shifted) * (-1.0 / (SPREAD * SPREAD * math.log(2.0))))
             inv_c = reciprocal(1.0 + bump)
-            rate = DELTA * inv_c
+            rate = (2.0 * DELTA) * inv_c
             t8 = t[0:8]
             h = hrow[pl.ds(p, 1)]
             code = crow[pl.ds(p, 1)]
@@ -214,26 +221,26 @@
             gain = 1.0 + dt * (bump * inv_c) * (shifted * (2.0 / (SPREAD * SPREAD)))
             gain = jnp.concatenate([gain[0:8] - jnp.where(top_row, rate[0:8] * h * slope, 0.0), gain[8:]], axis=0)
             gains[n, p] = gain
-            hcoef[n, pl.ds(p, 1)] = -(rate[0:8] * shape)[0:1]
+            hcoef[n, pl.ds(p, 1)] = (rate[0:8] * shape)[0:1]
             if n < steps - 1:
                 rates[n, p] = rate
                 after = t + dt
                 temps[n + 1, p] = after
-                keffs[n + 1, p] = kap[p] * active(acts[p], float(n + 1)) * (1.0 + 0.5 * after)
+                keffs[n + 1, p] = kap[p] * active(acts[p], float(n + 1)) * (2.0 + after)
             else:
                 mu[p] = lam[p] * rate
-            return fx
-
-        lax.fori_loop(0, planes, step, zero, unroll=UNROLL)
+            return fx, t_ahead, a_ahead
+
+        lax.fori_loop(0, planes, step, (zero,) + ahead(0), unroll=UNROLL)
 
     for n in range(steps):
         forward(n)
 
     def backward(n):
         def step(p, carry, store=None):
-            behind_e, behind_p = carry
+            behind_e, behind_p, m = carry
             t = temps[n, p]
-            m = mu[p]
+            m_ahead = mu[p + 1]
 
             def adjoint(axis, dm, ends):
                 if faces:
@@ -252,15 +259,15 @@
             def rolled(axis, count):
                 return lambda a: (pltpu.roll(a, count - 1, axis=axis), pltpu.roll(t, count - 1, axis=axis) - t)
 
-            ex, px, qx = adjoint(0, mu[p + 1] - m, lambda a: (keffs[n, p + 1], temps[n, p + 1] - t))
+            ex, px, qx = adjoint(0, m_ahead - m, lambda a: (keffs[n, p + 1], temps[n, p + 1] - t))
             ey, py, qy = adjoint(3, pltpu.roll(m, LANES - 1, axis=1) - m, rolled(1, LANES))
-            ez, pz, qz = adjoint(6, jnp.where(inner, pltpu.roll(m, rows - 1, axis=0) - m, 0.0), rolled(0, rows))
+            ez, pz, qz = adjoint(6, above_bottom(pltpu.roll(m, rows - 1, axis=0) - m), rolled(0, rows))
             energy = (ex - behind_e) + (ey - pltpu.roll(ey, 1, axis=1)) + (ez - pltpu.roll(ez, 1, axis=0))
             pull = (px + behind_p) + (py + pltpu.roll(qy, 1, axis=1)) + (pz + pltpu.roll(qz, 1, axis=0))
-            on = active(acts[p], float(n))
+            pull = pull * active(acts[p], float(n))
             old = lam[p]
-            new = old * gains[n, p] + 2.0 * energy - pull * (kap[p] * on)
-            grad = pull * (on * (2.0 + t))
+            new = old * gains[n, p] + energy - pull * kap[p]
+            grad = pull * (2.0 + t)
             hg = old[0:1] * hcoef[n, pl.ds(p, 1)]
             if n < steps - 1:
                 grad = kgrad[p] + grad
@@ -271,8 +278,8 @@
                 kgrad[p] = grad
                 hgrad[pl.ds(p, 1)] = hg
             else:
-                store(jnp.where(lane < HALF, new, pltpu.roll(-grad, HALF, axis=1)), hg)
-            return ex, qx
+                store(jnp.where(lane < HALF, new, pltpu.roll(-0.5 * grad, HALF, axis=1)), -0.5 * hg)
+            return ex, qx, m_ahead
 
         def last(i, carry):
             size = UNROLL * out_rows(rows)
@@ -287,9 +294,9 @@
             return carry
 
         if n > 0:
-            lax.fori_loop(0, planes, step, (zero, zero), unroll=UNROLL)
+            lax.fori_loop(0, planes, step, (zero, zero, mu[0]), unroll=UNROLL)
         else:
-            lax.fori_loop(0, planes // UNROLL, last, (zero, zero))
+            lax.fori_loop(0, planes // UNROLL, last, (zero, zero, mu[0]))
 
     for n in reversed(range(steps)):
         backward(n)

time: 48.8 us -> 48.6 us (level)
  no operation moved by 1% of the time
where the time goes in v4:
time: 48.6 us; the launch traced here: 48.4 us
  blocking collectives  38.6 us (79%)
  Pallas kernels  9.11 us (19%)
  between operations  0.65 us (1%)
    all_to_all x1, blocking collectives, body(): got = lax.all_to_all(packed, 'gx', 0, 0, tiled=True)  25.4 us
    all_to_all x1, blocking collectives, body(): lax.all_to_all(result, 'gx', 0, 0, tiled=True)  13.2 us
    pallas_call x1, Pallas kernels, body(): pl.pallas_call(compute, out_shape=jax.ShapeDtypeStruct((planes * out_rows...  6.75 us
    pallas_call x1, Pallas kernels, body(): pl.pallas_call(pack, out_shape=(jax.ShapeDtypeStruct((parts, in_rows(rows...  1.59 us

profile of v4, /device:TPU:0, one launch (start us, length us, event | category | flops | bytes accessed | tf_op | source)
XLA Modules:
  0.0 48.4 jit_solution(12071987675509699969)
XLA Ops:
  0.6 1.6 %shard_map.94 = (f32[16,80,128]{2,1,0:T(8,128)S(1)}, f32[4,16,128]{2,1,0:T(8,128)S(1)}) custom-call(s32[4,32]{1,0:T(4,128)} %refs_0_.1, f32[1,32,1024]{2,1,0:T(8,128)} %refs_1_.1, f32[1,32,1024]{2,1,0:T(8,128)} %refs_2_.1, s32[1,32,1024]{2,1,0:T(8,128)} %refs_3_.1, f32[1,1024]{1,0:T(1,128)} %refs_4_.1, s32[1,1024]{1,0:T(1,128)} %refs_5_.1, ...), custom_call_target="tpu_custom_call" | custom-call | tf_op jit(solution)/shard_map/pallas_call | solution.py:343
  2.2 25.4 %all_to_all.10.refs_0_ = f32[16,80,128]{2,1,0:T(8,128)S(1)} all-to-all(f32[16,80,128]{2,1,0:T(8,128)S(1)} %get-tuple-element.5), channel_id=1, replica_groups=mesh['groups'=2,'gx'=16] {'gx'}, dimensions={0} | all-to-all | bytes 1310720 | tf_op jit(solution)/shard_map/all_to_all | solution.py:356
  27.6 6.8 %shard_map.95 = f32[528,128]{1,0:T(8,128)S(1)} custom-call(f32[16,80,128]{2,1,0:T(8,128)S(1)} %all_to_all.10.refs_0_, f32[4,16,128]{2,1,0:T(8,128)S(1)} %get-tuple-element.6.refs_1_), custom_call_target="tpu_custom_call" | custom-call | tf_op jit(solution)/shard_map/pallas_call | solution.py:367
  34.4 13.2 %all_to_all.11 = f32[16,33,1,128]{3,2,1,0:T(1,128)S(1)} all-to-all(f32[16,33,1,128]{3,2,1,0:T(1,128)S(1)} %bitcast.3), channel_id=1, replica_groups=mesh['groups'=2,'gx'=16] {'gx'}, dimensions={0} | all-to-all | bytes 540672 | tf_op jit(solution)/shard_map/all_to_all | solution.py:391
  47.6 0.8 %shard_map.96 = (f32[1,32,1024]{2,1,0:T(8,128)}, f32[1,32,1024]{2,1,0:T(8,128)}, f32[1,1024]{1,0:T(1,128)}) custom-call(f32[528,128]{1,0:T(8,128)S(1)} %bitcast.2), custom_call_target="tpu_custom_call" | custom-call | tf_op jit(solution)/shard_map/pallas_call | solution.py:396

commit v5 on v4

--- a/solution.py
+++ b/solution.py
@@ -19,7 +19,7 @@
 LANES = 128
 HALF = 64
 LEFT = 96
-UNROLL = 8
+UNROLL = 16
 MIB = 1024 * 1024
 
 
@@ -124,129 +124,127 @@
 
 
 def window_kernel(
-    cols, width, got, heat, out, temps, keffs, rates, gains, kap, acts, lam, mu, kgrad, hcoef, hgrad, hrow, crow, *faces
+    cols, width, got, heat, out, temps, keffs, rates, gains, kap, acts, lam, mu, kgrad, hcoef, hrow, crow, *faces
 ):
     steps, planes = heat.shape[:2]
-    rows = temps.shape[2]
+    rows = kap.shape[0]
     half = rows // 2
+    unroll = UNROLL if planes <= 32 else 2
     base = lax.axis_index("gx") * width
-    lane = (lane_iota(rows) - lax.rem(base, LANES)) & (LANES - 1)
-    depth = lax.broadcasted_iota(jnp.int32, (rows, LANES), 0)
-    bottom = lax.broadcasted_iota(jnp.int32, (8, LANES), 0) == 7
-    top_row = lax.broadcasted_iota(jnp.int32, (8, LANES), 0) == 0
+    lane = (lane_iota(planes) - lax.rem(base, LANES)) & (LANES - 1)
+    end = lax.broadcasted_iota(jnp.int32, (8, LANES), 0) == 7
     column = base + jnp.where(lane < LEFT, lane, lane - LANES)
     inside = (column >= 0) & (column < cols)
-
-    place = jnp.where(lane[:8] < LEFT, lane[:8], lane[:8] - LANES) + 7 - 10 * (7 - depth[:8])
-    face_mask = (place >= 0) & (place < 10)
-
-    def above_bottom(value):
-        return jnp.concatenate([value[: rows - 8], jnp.where(bottom, 0.0, value[rows - 8 :])], axis=0)
+    zero = jnp.zeros((planes, LANES), jnp.float32)
+
+    def before_end(value):
+        return jnp.concatenate([value[: planes - 8], jnp.where(end, 0.0, value[planes - 8 :])], axis=0)
 
     def active(act, n):
         return jnp.where(act <= n, 1.0, 0.1)
 
-    def unpack(p, carry):
-        a = got[p, 0:rows]
-        b = got[p, rows : 2 * rows]
-        c = got[p, 2 * rows : 2 * rows + half]
-        temps[0, p] = a
-        k = jnp.where(inside, b, 0.0)
-        k = 0.5 * k
-        kap[p] = k
-        act = jnp.where(
-            (lane < 25) | (lane >= 121),
-            pltpu.roll(a, LANES - ACT_LOW, axis=1),
-            pltpu.roll(b, LANES - ACT_HIGH, axis=1),
-        )
-        acts[p] = act
-        cot = jnp.concatenate([c, pltpu.roll(c, HALF, axis=1)], axis=0)
-        cot = jnp.where(
-            lane < HALF,
-            cot,
-            jnp.where(lane < LEFT, pltpu.roll(a, LANES - COT_RIGHT, axis=1), pltpu.roll(a, LANES - COT_LEFT, axis=1)),
-        )
-        lam[p] = cot
-        face = pltpu.roll(a[0:16], 112, axis=1)
-        for bit in (1, 2, 4):
-            face = jnp.where((depth[:16] & bit) > 0, pltpu.roll(face, LANES - 10 * bit, axis=1), face)
-        hrow[pl.ds(p, 1)] = 0.5 * jnp.sum(jnp.where(face_mask, face[0:8], 0.0), axis=0, keepdims=True)
-        crow[pl.ds(p, 1)] = jnp.sum(jnp.where(face_mask, face[8:16], 0.0), axis=0, keepdims=True)
-        keffs[0, p] = k * active(act, 0.0) * (2.0 + a)
+    def layer(row):
+        return got[pl.ds(row, planes, stride=in_rows(rows))]
+
+    def unpack(q, carry):
+        c = layer(2 * rows + q)
+        for z, own in ((q, c), (q + half, pltpu.roll(c, HALF, axis=1))):
+            a = layer(z)
+            b = layer(rows + z)
+            temps[0, z] = a
+            k = 0.5 * jnp.where(inside, b, 0.0)
+            kap[z] = k
+            act = jnp.where(
+                (lane < 25) | (lane >= 121),
+                pltpu.roll(a, LANES - ACT_LOW, axis=1),
+                pltpu.roll(b, LANES - ACT_HIGH, axis=1),
+            )
+            acts[z] = act
+            lam[z] = jnp.where(
+                lane < HALF,
+                own,
+                jnp.where(
+                    lane < LEFT, pltpu.roll(a, LANES - COT_RIGHT, axis=1), pltpu.roll(a, LANES - COT_LEFT, axis=1)
+                ),
+            )
+            keffs[0, z] = k * active(act, 0.0) * (2.0 + a)
         return carry
 
-    lax.fori_loop(0, planes, unpack, 0, unroll=UNROLL)
-    zero = jnp.zeros((rows, LANES), jnp.float32)
+    lax.fori_loop(0, half, unpack, 0, unroll=unroll)
+
+    place = jnp.where(lane < LEFT, lane, lane - LANES) + 7
+    for held, first in ((hrow, 0), (crow, 8)):
+        value = zero
+        for r in range(8):
+            block = 10 * (7 - r)
+            moved = pltpu.roll(layer(first + r), LANES - (FACE + 7 - 70 + 10 * r), axis=1)
+            value = jnp.where((place >= block) & (place < block + 10), moved, value)
+        held[...] = value
     for n in range(steps):
-        temps[n, planes] = zero
-        keffs[n, planes] = zero
-    mu[planes] = zero
+        temps[n, rows] = zero
+        keffs[n, rows] = zero
+    mu[rows] = zero
 
     def forward(n):
-        def ahead(p):
-            return temps[n, p], keffs[n, p]
-
-        def step(p, carry):
+        top = temps[n, 0]
+        h = 0.5 * hrow[...]
+        square = top * top
+        radiative = crow[...] == 1.0
+        linear = top - jnp.where(crow[...] == 0.0, AMBIENT, SUBSTRATE)
+        shape = jnp.where(radiative, EMISSION * (square * square - AMBIENT**4), linear)
+        slope = jnp.where(radiative, 4.0 * EMISSION * square * top, 1.0)
+
+        def step(z, carry):
             behind, t, a = carry
-            t_ahead, a_ahead = ahead(p + 1)
+            t_ahead, a_ahead = temps[n, z + 1], keffs[n, z + 1]
 
             def flow(axis, b, dt):
                 first, second, positive = shares(a, b)
                 half_g = a * second
                 if faces:
-                    faces[0][n, axis, p] = half_g
-                    faces[0][n, axis + 1, p] = second * jnp.where(positive, second, 1.0) * dt
-                    faces[0][n, axis + 2, p] = first * jnp.where(positive, first, 1.0) * dt
+                    faces[0][n, axis, z] = half_g
+                    faces[0][n, axis + 1, z] = second * jnp.where(positive, second, 1.0) * dt
+                    faces[0][n, axis + 2, z] = first * jnp.where(positive, first, 1.0) * dt
                 return half_g * dt
 
-            fx = flow(0, a_ahead, t_ahead - t)
+            fz = flow(0, a_ahead, t_ahead - t)
             fy = flow(3, pltpu.roll(a, LANES - 1, axis=1), pltpu.roll(t, LANES - 1, axis=1) - t)
-            fz = flow(6, pltpu.roll(a, rows - 1, axis=0), above_bottom(pltpu.roll(t, rows - 1, axis=0) - t))
-            flux = (fx - behind) + (fy - pltpu.roll(fy, 1, axis=1)) + (fz - pltpu.roll(fz, 1, axis=0))
+            fx = flow(6, pltpu.roll(a, planes - 1, axis=0), before_end(pltpu.roll(t, planes - 1, axis=0) - t))
+            flux = (fz - behind) + (fy - pltpu.roll(fy, 1, axis=1)) + (fx - pltpu.roll(fx, 1, axis=0))
             shifted = t - MELT
             bump = LATENT * jnp.exp2(jnp.square(shifted) * (-1.0 / (SPREAD * SPREAD * math.log(2.0))))
             inv_c = reciprocal(1.0 + bump)
             rate = (2.0 * DELTA) * inv_c
-            t8 = t[0:8]
-            h = hrow[pl.ds(p, 1)]
-            code = crow[pl.ds(p, 1)]
-            square = t8 * t8
-            radiative = code == 1.0
-            linear = t8 - jnp.where(code == 0.0, AMBIENT, SUBSTRATE)
-            shape = jnp.where(radiative, EMISSION * (square * square - AMBIENT**4), linear)
-            slope = jnp.where(radiative, 4.0 * EMISSION * square * t8, 1.0)
-            surface = jnp.where(top_row, heat[n, pl.ds(p, 1)] - h * shape, 0.0)
-            flux = jnp.concatenate([flux[0:8] + surface, flux[8:]], axis=0)
             dt = flux * rate
-            gain = 1.0 + dt * (bump * inv_c) * (shifted * (2.0 / (SPREAD * SPREAD)))
-            gain = jnp.concatenate([gain[0:8] - jnp.where(top_row, rate[0:8] * h * slope, 0.0), gain[8:]], axis=0)
-            gains[n, p] = gain
-            hcoef[n, pl.ds(p, 1)] = (rate[0:8] * shape)[0:1]
+            gains[n, z] = 1.0 + dt * (bump * inv_c) * (shifted * (2.0 / (SPREAD * SPREAD)))
+            rates[n, z] = rate
             if n < steps - 1:
-                rates[n, p] = rate
                 after = t + dt
-                temps[n + 1, p] = after
-                keffs[n + 1, p] = kap[p] * active(acts[p], float(n + 1)) * (2.0 + after)
+                temps[n + 1, z] = after
+                keffs[n + 1, z] = kap[z] * active(acts[z], float(n + 1)) * (2.0 + after)
             else:
-                mu[p] = lam[p] * rate
-            return fx, t_ahead, a_ahead
-
-        lax.fori_loop(0, planes, step, (zero,) + ahead(0), unroll=UNROLL)
+                mu[z] = lam[z] * rate
+            return fz, t_ahead, a_ahead
+
+        lax.fori_loop(0, rows, step, (h * shape - heat[n], top, keffs[n, 0]), unroll=unroll)
+        rate = rates[n, 0]
+        gains[n, 0] = gains[n, 0] - rate * h * slope
+        hcoef[n] = rate * shape
 
     for n in range(steps):
         forward(n)
 
     def backward(n):
-        def step(p, carry, store=None):
+        def step(z, carry):
             behind_e, behind_p, m = carry
-            t = temps[n, p]
-            m_ahead = mu[p + 1]
+            t = temps[n, z]
+            m_ahead = mu[z + 1]
 
             def adjoint(axis, dm, ends):
                 if faces:
-                    half_g, first, second = (faces[0][n, axis + i, p] for i in range(3))
+                    half_g, first, second = (faces[0][n, axis + i, z] for i in range(3))
                     return half_g * dm, first * dm, second * dm
-                a = keffs[n, p]
+                a = keffs[n, z]
                 b, dt = ends(a)
                 first, second, positive = shares(a, b)
                 q = dt * dm
@@ -259,47 +257,33 @@
             def rolled(axis, count):
                 return lambda a: (pltpu.roll(a, count - 1, axis=axis), pltpu.roll(t, count - 1, axis=axis) - t)
 
-            ex, px, qx = adjoint(0, m_ahead - m, lambda a: (keffs[n, p + 1], temps[n, p + 1] - t))
+            ez, pz, qz = adjoint(0, m_ahead - m, lambda a: (keffs[n, z + 1], temps[n, z + 1] - t))
             ey, py, qy = adjoint(3, pltpu.roll(m, LANES - 1, axis=1) - m, rolled(1, LANES))
-            ez, pz, qz = adjoint(6, above_bottom(pltpu.roll(m, rows - 1, axis=0) - m), rolled(0, rows))
-            energy = (ex - behind_e) + (ey - pltpu.roll(ey, 1, axis=1)) + (ez - pltpu.roll(ez, 1, axis=0))
-            pull = (px + behind_p) + (py + pltpu.roll(qy, 1, axis=1)) + (pz + pltpu.roll(qz, 1, axis=0))
-            pull = pull * active(acts[p], float(n))
-            old = lam[p]
-            new = old * gains[n, p] + energy - pull * kap[p]
+            ex, px, qx = adjoint(6, before_end(pltpu.roll(m, planes - 1, axis=0) - m), rolled(0, planes))
+            energy = (ez - behind_e) + (ey - pltpu.roll(ey, 1, axis=1)) + (ex - pltpu.roll(ex, 1, axis=0))
+            pull = (pz + behind_p) + (py + pltpu.roll(qy, 1, axis=1)) + (px + pltpu.roll(qx, 1, axis=0))
+            pull = pull * active(acts[z], float(n))
+            new = lam[z] * gains[n, z] + energy - pull * kap[z]
             grad = pull * (2.0 + t)
-            hg = old[0:1] * hcoef[n, pl.ds(p, 1)]
             if n < steps - 1:
-                grad = kgrad[p] + grad
-                hg = hgrad[pl.ds(p, 1)] + hg
+                grad = kgrad[z] + grad
             if n > 0:
-                lam[p] = new
-                mu[p] = new * rates[n - 1, p]
-                kgrad[p] = grad
-                hgrad[pl.ds(p, 1)] = hg
+                lam[z] = new
+                mu[z] = new * rates[n - 1, z]
+                kgrad[z] = grad
             else:
-                store(jnp.where(lane < HALF, new, pltpu.roll(-0.5 * grad, HALF, axis=1)), -0.5 * hg)
-            return ex, qx, m_ahead
-
-        def last(i, carry):
-            size = UNROLL * out_rows(rows)
-            chunk = out.at[pl.ds(pl.multiple_of(i * size, 8), size)]
-            for j in range(UNROLL):
-
-                def store(cube, row, at=j * out_rows(rows)):
-                    chunk[at : at + rows] = cube
-                    chunk[at + rows : at + rows + 1] = row
-
-                carry = step(i * UNROLL + j, carry, store)
-            return carry
-
-        if n > 0:
-            lax.fori_loop(0, planes, step, (zero, zero, mu[0]), unroll=UNROLL)
-        else:
-            lax.fori_loop(0, planes // UNROLL, last, (zero, zero, mu[0]))
-
+                out[pl.ds(z, planes, stride=out_rows(rows))] = jnp.where(
+                    lane < HALF, new, pltpu.roll(-0.5 * grad, HALF, axis=1)
+                )
+            return ez, qz, m_ahead
+
+        lax.fori_loop(0, rows, step, (zero, zero, mu[0]), unroll=unroll)
+
+    total = zero
     for n in reversed(range(steps)):
+        total = total + lam[0] * hcoef[n]
         backward(n)
+    out[pl.ds(rows, planes, stride=out_rows(rows))] = -0.5 * total
 
 
 def unpack_kernel(width, got, adjoint, kgrad, hgrad):
@@ -361,7 +345,7 @@
     keep = 9 * steps if planes <= 32 else 0
 
     def held(count, extra=0):
-        return pltpu.VMEM(count + (planes + extra, rows, LANES), jnp.float32)
+        return pltpu.VMEM(count + (rows + extra, planes, LANES), jnp.float32)
 
     row = pltpu.VMEM((planes, LANES), jnp.float32)
     result = pl.pallas_call(
@@ -372,7 +356,7 @@
         scratch_shapes=[
             held((steps,), 1),
             held((steps,), 1),
-            held((steps - 1,)),
+            held((steps,)),
             held((steps,)),
             held(()),
             held(()),
@@ -382,11 +366,10 @@
             pltpu.VMEM((steps, planes, LANES), jnp.float32),
             row,
             row,
-            row,
         ]
         + ([held((steps, 9))] if keep else []),
         compiler_params=params(planes * ((24 + keep) * plane + (in_rows(rows) + out_rows(rows)) * LANES)),
-    )(got, heat)
+    )(got.reshape(planes * in_rows(rows), LANES), heat)
     result = result.reshape(planes, out_rows(rows), 1, LANES)
     back = lax.all_to_all(result, "gx", 0, 0, tiled=True).reshape(planes * out_rows(rows), LANES)
 

time: 48.6 us -> 47.9 us (0.986)
  Pallas kernels: 9.11 us -> 8.4 us
    pallas_call x1, Pallas kernels: 6.75 us -> 6.04 us  [body(): pl.pallas_call(compute, out_shape=jax.ShapeDtypeStruct((planes * out_rows...]
where the time goes in v5:
time: 47.9 us; the launch traced here: 47.7 us
  blocking collectives  38.6 us (81%)
  Pallas kernels  8.4 us (18%)
  between operations  0.65 us (1%)
    all_to_all x1, blocking collectives, body(): got = lax.all_to_all(packed, 'gx', 0, 0, tiled=True)  25.4 us
    all_to_all x1, blocking collectives, body(): lax.all_to_all(result, 'gx', 0, 0, tiled=True)  13.2 us
    pallas_call x1, Pallas kernels, body(): pl.pallas_call(compute, out_shape=jax.ShapeDtypeStruct((planes * out_rows...  6.04 us
    pallas_call x1, Pallas kernels, body(): pl.pallas_call(pack, out_shape=(jax.ShapeDtypeStruct((parts, in_rows(rows...  1.59 us

profile of v5, /device:TPU:0, one launch (start us, length us, event | category | flops | bytes accessed | tf_op | source)
XLA Modules:
  0.0 47.7 jit_solution(8297959130811043675)
XLA Ops:
  0.6 1.6 %shard_map.94 = (f32[16,80,128]{2,1,0:T(8,128)S(1)}, f32[4,16,128]{2,1,0:T(8,128)S(1)}) custom-call(s32[4,32]{1,0:T(4,128)} %refs_0_.1, f32[1,32,1024]{2,1,0:T(8,128)} %refs_1_.1, f32[1,32,1024]{2,1,0:T(8,128)} %refs_2_.1, s32[1,32,1024]{2,1,0:T(8,128)} %refs_3_.1, f32[1,1024]{1,0:T(1,128)} %refs_4_.1, s32[1,1024]{1,0:T(1,128)} %refs_5_.1, ...), custom_call_target="tpu_custom_call" | custom-call | tf_op jit(solution)/shard_map/pallas_call | solution.py:327
  2.2 25.4 %all_to_all.10 = f32[16,80,128]{2,1,0:T(8,128)S(1)} all-to-all(f32[16,80,128]{2,1,0:T(8,128)S(1)} %get-tuple-element.5), channel_id=1, replica_groups=mesh['groups'=2,'gx'=16] {'gx'}, dimensions={0} | all-to-all | bytes 1310720 | tf_op jit(solution)/shard_map/all_to_all | solution.py:340
  27.6 6.0 %shard_map.95 = f32[528,128]{1,0:T(8,128)S(1)} custom-call(f32[1280,128]{1,0:T(8,128)S(1)} %bitcast.3, f32[4,16,128]{2,1,0:T(8,128)S(1)} %get-tuple-element.6.refs_1_), custom_call_target="tpu_custom_call" | custom-call | tf_op jit(solution)/shard_map/pallas_call | solution.py:351
  33.7 13.2 %all_to_all.11 = f32[16,33,1,128]{3,2,1,0:T(1,128)S(1)} all-to-all(f32[16,33,1,128]{3,2,1,0:T(1,128)S(1)} %bitcast.5), channel_id=1, replica_groups=mesh['groups'=2,'gx'=16] {'gx'}, dimensions={0} | all-to-all | bytes 540672 | tf_op jit(solution)/shard_map/all_to_all | solution.py:374
  46.9 0.8 %shard_map.96 = (f32[1,32,1024]{2,1,0:T(8,128)}, f32[1,32,1024]{2,1,0:T(8,128)}, f32[1,1024]{1,0:T(1,128)}) custom-call(f32[528,128]{1,0:T(8,128)S(1)} %bitcast.4), custom_call_target="tpu_custom_call" | custom-call | tf_op jit(solution)/shard_map/pallas_call | solution.py:379

commit v6 on v5

--- a/solution.py
+++ b/solution.py
@@ -27,11 +27,11 @@
     return lax.broadcasted_iota(jnp.int32, (rows, LANES), 1)
 
 
-ACT_LOW, ACT_HIGH, COT_RIGHT, COT_LEFT, FACE = 96, 50, 11, 75, 79
+ACT_LOW, ACT_HIGH, COT_RIGHT, COT_LEFT = 96, 50, 11, 75
 
 
 def in_rows(rows):
-    return 2 * rows + rows // 2
+    return 2 * rows + rows // 2 + 2
 
 
 def out_rows(rows):
@@ -41,7 +41,7 @@
 def pack_kernel(parts, width, *refs):
     path, *sources = refs[:7]
     out, heat = refs[7:9]
-    spots, temp, kappa, act, hface, codes, cot, faces, done = refs[9:]
+    spots, temp, kappa, act, hface, codes, cot, done = refs[9:]
     cols = temp.shape[-1]
     rows = temp.shape[1]
     half = rows // 2
@@ -68,9 +68,6 @@
 
     for copy in copies[1:]:
         copy.wait()
-    faces[0:8] = jnp.broadcast_to(hface[...], (8, cols))
-    faces[8:16] = jnp.broadcast_to(codes[...].astype(jnp.float32), (8, cols))
-
     lane_of = lane_iota(rows)
     for d in range(parts):
         tile, off = divmod(d * width, LANES)
@@ -94,22 +91,19 @@
         k = window(kappa)
         a = window(act)
         c = window(cot)
-        face = window(faces)
         extra = jnp.where(
             lane >= 89,
             pltpu.roll(a, ACT_LOW, axis=1),
             jnp.where(lane >= 75, pltpu.roll(c, COT_RIGHT, axis=1), pltpu.roll(c, COT_LEFT, axis=1)),
         )
-        face = jnp.concatenate(
-            [pltpu.roll(x, FACE + 7 - 70, axis=1, stride=10, stride_axis=0) for x in (face[0:8], face[8:16])], axis=0
-        )
-        face = jnp.where((lane[:16] >= FACE) & (lane[:16] < 89), face, extra[:16])
-        extra = jnp.concatenate([face, extra[16:]], axis=0)
-        out[d, 0:rows] = jnp.where((lane >= 71) & (lane < 121), extra, t)
-        out[d, rows : 2 * rows] = jnp.where((lane >= 75) & (lane < 121), pltpu.roll(a, ACT_HIGH, axis=1), k)
-        out[d, 2 * rows : 2 * rows + half] = jnp.where(
+        at = d * in_rows(rows)
+        out[at : at + rows] = jnp.where((lane >= 71) & (lane < 121), extra, t)
+        out[at + rows : at + 2 * rows] = jnp.where((lane >= 75) & (lane < 121), pltpu.roll(a, ACT_HIGH, axis=1), k)
+        out[at + 2 * rows : at + 2 * rows + half] = jnp.where(
             lane[:half] < HALF, c[:half], pltpu.roll(c[half:], HALF, axis=1)
         )
+        out[at + 2 * rows + half : at + 2 * rows + half + 1] = window(hface)
+        out[at + 2 * rows + half + 1 : at + 2 * rows + half + 2] = window(codes)
 
 
 def reciprocal(value):
@@ -172,14 +166,8 @@
 
     lax.fori_loop(0, half, unpack, 0, unroll=unroll)
 
-    place = jnp.where(lane < LEFT, lane, lane - LANES) + 7
-    for held, first in ((hrow, 0), (crow, 8)):
-        value = zero
-        for r in range(8):
-            block = 10 * (7 - r)
-            moved = pltpu.roll(layer(first + r), LANES - (FACE + 7 - 70 + 10 * r), axis=1)
-            value = jnp.where((place >= block) & (place < block + 10), moved, value)
-        held[...] = value
+    hrow[...] = layer(2 * rows + half)
+    crow[...] = layer(2 * rows + half + 1)
     for n in range(steps):
         temps[n, rows] = zero
         keffs[n, rows] = zero
@@ -212,11 +200,10 @@
             fx = flow(6, pltpu.roll(a, planes - 1, axis=0), before_end(pltpu.roll(t, planes - 1, axis=0) - t))
             flux = (fz - behind) + (fy - pltpu.roll(fy, 1, axis=1)) + (fx - pltpu.roll(fx, 1, axis=0))
             shifted = t - MELT
-            bump = LATENT * jnp.exp2(jnp.square(shifted) * (-1.0 / (SPREAD * SPREAD * math.log(2.0))))
-            inv_c = reciprocal(1.0 + bump)
-            rate = (2.0 * DELTA) * inv_c
+            bump = (0.5 * LATENT / DELTA) * jnp.exp2(jnp.square(shifted) * (-1.0 / (SPREAD * SPREAD * math.log(2.0))))
+            rate = reciprocal(0.5 / DELTA + bump)
             dt = flux * rate
-            gains[n, z] = 1.0 + dt * (bump * inv_c) * (shifted * (2.0 / (SPREAD * SPREAD)))
+            gains[n, z] = 1.0 + dt * (bump * rate) * (shifted * (2.0 / (SPREAD * SPREAD)))
             rates[n, z] = rate
             if n < steps - 1:
                 after = t + dt
@@ -327,16 +314,17 @@
     packed, heat = pl.pallas_call(
         pack,
         out_shape=(
-            jax.ShapeDtypeStruct((parts, in_rows(rows), LANES), jnp.float32),
+            jax.ShapeDtypeStruct((parts * in_rows(rows), LANES), jnp.float32),
             jax.ShapeDtypeStruct((steps, planes, LANES), jnp.float32),
         ),
         in_specs=[hbm] * 7,
         out_specs=(vmem, vmem),
         scratch_shapes=[pltpu.SMEM(path.shape, path.dtype)]
         + [pltpu.VMEM(x.shape, x.dtype) for x in sources]
-        + [pltpu.VMEM((16, cols), jnp.float32), pltpu.SemaphoreType.DMA((7,))],
+        + [pltpu.SemaphoreType.DMA((7,))],
         compiler_params=params(5 * rows * cols + parts * (in_rows(rows) + steps) * LANES),
     )(*[pltpu.with_memory_space_constraint(x, pltpu.HBM) for x in (path,) + sources])
+    packed = packed.reshape(parts, in_rows(rows), 1, LANES)
     got = lax.all_to_all(packed, "gx", 0, 0, tiled=True)
 
     def compute(*refs):

time: 47.9 us -> 48.1 us (level)
  no operation moved by 1% of the time
where the time goes in v6:
time: 48.1 us; the launch traced here: 47.9 us
  blocking collectives  38.9 us (81%)
  Pallas kernels  8.31 us (17%)
  between operations  0.65 us (1%)
    all_to_all x1, blocking collectives, body(): got = lax.all_to_all(packed, 'gx', 0, 0, tiled=True)  25.6 us
    all_to_all x1, blocking collectives, body(): lax.all_to_all(result, 'gx', 0, 0, tiled=True)  13.4 us
    pallas_call x1, Pallas kernels, body(): pl.pallas_call(compute, out_shape=jax.ShapeDtypeStruct((planes * out_rows...  5.99 us
    pallas_call x1, Pallas kernels, body(): pl.pallas_call(pack, out_shape=(jax.ShapeDtypeStruct((parts * in_rows(row...  1.56 us

profile of v6, /device:TPU:0, one launch (start us, length us, event | category | flops | bytes accessed | tf_op | source)
XLA Modules:
  0.0 47.9 jit_solution(15908541028563168146)
XLA Ops:
  0.6 1.6 %shard_map.94 = (f32[1312,128]{1,0:T(8,128)S(1)}, f32[4,16,128]{2,1,0:T(8,128)S(1)}) custom-call(s32[4,32]{1,0:T(4,128)} %refs_0_.1, f32[1,32,1024]{2,1,0:T(8,128)} %refs_1_.1, f32[1,32,1024]{2,1,0:T(8,128)} %refs_2_.1, s32[1,32,1024]{2,1,0:T(8,128)} %refs_3_.1, f32[1,1024]{1,0:T(1,128)} %refs_4_.1, s32[1,1024]{1,0:T(1,128)} %refs_5_.1, f32[1,32,1024]{2,1,0:T(8,128)} %refs_6_.1), custom_call_target="tpu_custom_call" | custom-call | tf_op jit(solution)/shard_map/pallas_call | solution.py:314
  2.2 25.6 %all_to_all.10 = f32[16,82,1,128]{3,2,1,0:T(1,128)S(1)} all-to-all(f32[16,82,1,128]{3,2,1,0:T(1,128)S(1)} %bitcast.7), channel_id=1, replica_groups=mesh['groups'=2,'gx'=16] {'gx'}, dimensions={0} | all-to-all | bytes 1343488 | tf_op jit(solution)/shard_map/all_to_all | solution.py:328
  27.8 6.0 %shard_map.95 = f32[528,128]{1,0:T(8,128)S(1)} custom-call(f32[1312,128]{1,0:T(8,128)S(1)} %bitcast.4, f32[4,16,128]{2,1,0:T(8,128)S(1)} %get-tuple-element.6.refs_1_), custom_call_target="tpu_custom_call" | custom-call | tf_op jit(solution)/shard_map/pallas_call | solution.py:339
  33.8 13.4 %all_to_all.11 = f32[16,33,1,128]{3,2,1,0:T(1,128)S(1)} all-to-all(f32[16,33,1,128]{3,2,1,0:T(1,128)S(1)} %bitcast.6), channel_id=1, replica_groups=mesh['groups'=2,'gx'=16] {'gx'}, dimensions={0} | all-to-all | bytes 540672 | tf_op jit(solution)/shard_map/all_to_all | solution.py:362
  47.1 0.8 %shard_map.96 = (f32[1,32,1024]{2,1,0:T(8,128)}, f32[1,32,1024]{2,1,0:T(8,128)}, f32[1,1024]{1,0:T(1,128)}) custom-call(f32[528,128]{1,0:T(8,128)S(1)} %bitcast.5), custom_call_target="tpu_custom_call" | custom-call | tf_op jit(solution)/shard_map/pallas_call | solution.py:367
